TPU v7x, 512 devices: a whole 4x8x8 slice. The times are simulated.
512 devices in a mesh: pair: 32 (over x, y), row: 16 (over z, core).
Axes of the slice: x: 4, y: 8, z: 8, core: 2. Of those that a mesh axis runs over, the one named last changes fastest.
Arguments:
- activations: float32 [32768, 8192], P('row', 'pair'), may hold values from -32 to 32
Outputs:
- rotated: float32 [32768, 8192], P('row', 'pair')
All inputs are finite; a program needn't handle non-finite values.
Results may differ from a plain program's by a relative error of at most 0.0003.
Values sent between devices are 32-bit elements; how exact they have to be, the bound alone decides.
No kernel may reach another device: no remote copies, remote signals or barrier semaphores. Data moves between devices by JAX's collectives and lax.ppermute only.
A program may use at most 64 MiB of HBM per device.

v0:
```python
import jax
import jax.numpy as jnp
from jax import lax
from jax.sharding import PartitionSpec as P

STEPS = 16


def passed_along(value, axis, steps):
    count = lax.axis_size(axis)
    pairs = [(source, (source + steps) % count) for source in range(count)]
    return lax.ppermute(value, axis, pairs)


def turn_columns(matrix, cos_part, sin_part, half_size):
    upper_part = matrix[:, :half_size]
    lower_part = matrix[:, half_size:]
    return jnp.concatenate(
        (
            upper_part * cos_part + lower_part * sin_part,
            lower_part * cos_part - upper_part * sin_part,
        ),
        axis=1,
    )


def turn_rows(matrix, cos_part, sin_part, half_size):
    upper_part = matrix[:half_size, :]
    lower_part = matrix[half_size:, :]
    cos_col = cos_part[:, None]
    sin_col = sin_part[:, None]
    return jnp.concatenate(
        (upper_part * cos_col + lower_part * sin_col, lower_part * cos_col - upper_part * sin_col),
        axis=0,
    )


def roll_lower(matrix, dim_axis, half_size, offset_by):
    if dim_axis == 0:
        return jnp.concatenate(
            (matrix[:half_size], jnp.roll(matrix[half_size:], offset_by, axis=0)), axis=0
        )
    return jnp.concatenate(
        (matrix[:, :half_size], jnp.roll(matrix[:, half_size:], offset_by, axis=1)), axis=1
    )


def diagonal_mask(order_size):
    row_ids = lax.broadcasted_iota(jnp.int32, (order_size, order_size), 0)
    col_ids = lax.broadcasted_iota(jnp.int32, (order_size, order_size), 1)
    return (row_ids == col_ids).astype(jnp.float32)


def masked_diagonal(matrix, mask_table):
    return jnp.sum(matrix * mask_table, axis=0)


def jacobi_rotations(gram_matrix, step_count):
    half_size = gram_matrix.shape[0] // 2
    full_mask = diagonal_mask(2 * half_size)
    half_mask = diagonal_mask(half_size)

    def one_step(step_idx, carried):
        gram_now, rotation = carried
        diag_vals = masked_diagonal(gram_now, full_mask)
        upper_diag = diag_vals[:half_size]
        lower_diag = diag_vals[half_size:]
        coupling = masked_diagonal(gram_now[:half_size, half_size:], half_mask)
        rot_angle = 0.5 * jnp.arctan2(2.0 * coupling, upper_diag - lower_diag)
        cos_part = jnp.cos(rot_angle)
        sin_part = jnp.sin(rot_angle)
        gram_now = turn_rows(
            turn_columns(gram_now, cos_part, sin_part, half_size), cos_part, sin_part, half_size
        )
        rotation = turn_columns(rotation, cos_part, sin_part, half_size)
        gram_now = roll_lower(roll_lower(gram_now, 0, half_size, 1), 1, half_size, 1)
        rotation = roll_lower(rotation, 1, half_size, 1)
        return (gram_now, rotation)

    start = (gram_matrix, full_mask)
    gram_end, rotation = lax.fori_loop(0, step_count, one_step, start)
    return roll_lower(rotation, 1, half_size, -step_count)


def products(left_cols, right_cols):
    return jnp.dot(left_cols.T, right_cols, precision=lax.Precision.HIGHEST)


def summed_gram(pair_cols):
    return lax.psum(products(pair_cols, pair_cols), "row")


def body(activations):
    half_size = activations.shape[1] // 2
    entry_count = (
        activations.shape[0] * activations.shape[1] * lax.axis_size("pair") * lax.axis_size("row")
    )
    sum_squares = lax.psum(jnp.sum(activations * activations), ("pair", "row"))
    gram_one = summed_gram(activations)
    rotation_one = jacobi_rotations(gram_one, STEPS)
    rotated_one = jnp.dot(activations, rotation_one, precision=lax.Precision.HIGHEST)
    upper_one = rotated_one[:, :half_size]
    lower_one = rotated_one[:, half_size:]
    arrived = passed_along(lower_one, "pair", 1)
    pair_two = jnp.concatenate((upper_one, arrived), axis=1)
    gram_two = summed_gram(pair_two)
    rotation_two = jacobi_rotations(gram_two, STEPS)
    rotated_two = jnp.dot(pair_two, rotation_two, precision=lax.Precision.HIGHEST)
    rms_value = jnp.sqrt(sum_squares / entry_count)
    return rotated_two / rms_value


def solution(mesh):
    in_specs = (P("row", "pair"),)
    out_specs = P("row", "pair")
    return jax.shard_map(body, mesh=mesh, in_specs=in_specs, out_specs=out_specs, check_vma=False)
```

profile of v0, /device:TPU:1, one launch (start us, length us, event | category | flops | bytes accessed | tf_op | source)
XLA Modules:
  0.0 429.6 jit_solution(14587510920593654217)
XLA Ops:
  6.5 6.4 %fusion.28 = f32[256,256]{1,0:T(8,128)} fusion(f32[2048,256]{1,0:T(8,128)} %param.5), kind=kOutput, calls=%fused_computation.63 | convolution fusion | flops 1610612736 | bytes 2359296 | tf_op jit(solution)/shard_map/dot_general | solution.py:86
  13.1 120.2 %all-reduce.3.cloned.1.call-done = f32[256,256]{1,0:T(8,128)} async-done(((f32[256,256]{1,0:T(8,128)}), f32[256,256]{1,0:T(8,128)}) %all-reduce.3.cloned.1.call-update) | async-done | bytes 262160 | tf_op jit(solution)/shard_map/psum | solution.py:90
  133.2 67.8 %while.26 = (s32[]{:T(128)}, f32[256,256]{1,0:T(8,128)}, f32[256,256]{1,0:T(8,128)S(1)}, s32[]{:T(128)}) while((s32[]{:T(128)}, f32[256,256]{1,0:T(8,128)}, f32[256,256]{1,0:T(8,128)S(1)}, s32[]{:T(128)}) %tuple.68), condition=%wide.region_4.5_spmd.clone, body=%wide.region_1.4_spmd.clone.sunk | while | flops 1327106 | bytes 4009013 | solution.py:81
  133.2 1.0 select_reduce_fusion.9
  134.2 1.0 select_reduce_fusion.8
  135.4 1.0 multiply_add_fusion.10
  139.6 1.0 multiply_add_fusion.10
  143.8 1.0 multiply_add_fusion.10
  148.0 1.0 multiply_add_fusion.10
  152.3 1.0 multiply_add_fusion.10
  156.5 1.0 multiply_add_fusion.10
  160.7 1.0 multiply_add_fusion.10
  163.8 1.0 select_reduce_fusion.8
  165.0 1.0 multiply_add_fusion.10
  169.2 1.0 multiply_add_fusion.10
  173.4 1.0 multiply_add_fusion.10
  177.6 1.0 multiply_add_fusion.10
  181.9 1.0 multiply_add_fusion.10
  186.1 1.0 multiply_add_fusion.10
  190.3 1.0 multiply_add_fusion.10
  194.6 1.0 multiply_add_fusion.10
  198.8 1.0 multiply_add_fusion.10
  201.2 3.6 convolution_bitcast_fusion
  205.0 3.1 collective-permute-start
  208.1 26.2 %collective-permute-done = f32[2048,128]{0,1:T(8,128)S(1)} collective-permute-done((f32[2048,128]{0,1:T(8,128)S(1)}, f32[2048,128]{0,1:T(8,128)S(1)}, u32[]{:S(2)}, u32[]{:S(2)}) %collective-permute-start) | collective-permute-done | bytes 1048608 | tf_op jit(solution)/shard_map/ppermute | solution.py:12
  235.3 2.6 fusion.10
  237.9 1.1 multiply_reduce_fusion
  239.0 96.0 %psum.23 = f32[]{:T(128)} all-reduce(f32[]{:T(128)} %multiply_reduce_fusion), channel_id=1, replica_groups=mesh['pair'=32,'row'=16] {'pair','row'}, use_global_device_ids=true, to_apply=%region_11.12 | all-reduce | flops 1 | bytes 8 | tf_op jit(solution)/shard_map/psum | solution.py:98
  335.6 14.5 %all-reduce.5.cloned.1.call-done = f32[256,256]{1,0:T(8,128)} async-done(((f32[256,256]{1,0:T(8,128)}), f32[256,256]{1,0:T(8,128)}) %all-reduce.5.cloned.1.call-update) | async-done | bytes 262160 | tf_op jit(solution)/shard_map/psum | solution.py:90
  350.1 67.7 %while.27 = (s32[]{:T(128)}, f32[256,256]{1,0:T(8,128)}, f32[256,256]{1,0:T(8,128)S(1)}, s32[]{:T(128)}) while((s32[]{:T(128)}, f32[256,256]{1,0:T(8,128)}, f32[256,256]{1,0:T(8,128)S(1)}, s32[]{:T(128)}) %tuple.71), condition=%wide.region_9.10_spmd.clone, body=%wide.region_6.0_spmd.clone.sunk | while | flops 1327106 | bytes 4009013 | solution.py:81
  352.2 1.0 multiply_add_fusion.12
  355.3 1.0 select_reduce_fusion.10
  356.4 1.0 multiply_add_fusion.12
  360.6 1.0 multiply_add_fusion.12
  364.8 1.0 multiply_add_fusion.12
  369.1 1.0 multiply_add_fusion.12
  373.3 1.0 multiply_add_fusion.12
  377.5 1.0 multiply_add_fusion.12
  381.8 1.0 multiply_add_fusion.12
  386.0 1.0 multiply_add_fusion.12
  390.2 1.0 multiply_add_fusion.12
  394.4 1.0 multiply_add_fusion.12
  398.7 1.0 multiply_add_fusion.12
  402.9 1.0 multiply_add_fusion.12
  407.1 1.0 multiply_add_fusion.12
  411.4 1.0 multiply_add_fusion.12
  415.6 1.0 multiply_add_fusion.12
  418.0 4.8 %convolution_divide_fusion = f32[2048,256]{1,0:T(8,128)} fusion(f32[2048,128]{0,1:T(8,128)S(1)} %copy-done.2, f32[2048,128]{0,1:T(8,128)S(1)} %get-tuple-element.115, f32[]{:T(128)S(6)} %sqrt.3, f32[256,16]{1,0:T(8,128)S(1)} %slice.145, f32[256,112]{1,0:T(8,128)S(1)} %slice.144, f32[256,128]{1,0:T(8,128)S(1)} %slice.143), kind=kOutput, calls=%fused_computation.41 | convolution fusion | flops 1611792384 | bytes 4456452 | tf_op jit(solution)/shard_map/dot_general | solution.py:108
  (399 shorter events, 98.0 us)
Async XLA Ops:
  6.5 126.7 %all-reduce.3.cloned.1.call-start = ((), (), s32[]{:S(2)}) async-start(), calls=%async_computation | async-start | bytes 524288 | tf_op jit(solution)/shard_map/psum | solution.py:90
  13.0 337.1 %all-reduce.5.cloned.1.call-start = ((), (), s32[]{:S(2)}) async-start(), calls=%async_computation.1 | async-start | bytes 524288 | tf_op jit(solution)/shard_map/psum | solution.py:90
  133.2 67.9 %copy-start = (f32[2048,256]{1,0:T(8,128)S(1)}, f32[2048,256]{1,0:T(8,128)}, u32[]{:S(2)}) copy-start(f32[2048,256]{1,0:T(8,128)} %param.5) | copy-start | bytes 6291460
  205.0 29.3 %collective-permute-start = (f32[2048,128]{0,1:T(8,128)S(1)}, f32[2048,128]{0,1:T(8,128)S(1)}, u32[]{:S(2)}, u32[]{:S(2)}) collective-permute-start(f32[2048,128]{0,1:T(8,128)S(1)} %get-tuple-element.116), channel_id=1, source_target_pairs={{0,16},{16,32},{32,48},{48,64},{64,80},{80,96},{96,112},{112,128},... | collective-permute-start | bytes 3145736 | tf_op jit(solution)/shard_map/ppermute | solution.py:12
  234.3 1.0 copy-start.1
  350.1 67.9 %copy-start.2 = (f32[2048,128]{0,1:T(8,128)S(1)}, f32[2048,128]{0,1:T(8,128)}, u32[]{:S(2)}) copy-start(f32[2048,128]{0,1:T(8,128)} %copy-done.1) | copy-start | bytes 3145732
Sparse Core Ops, SparseCore 0:
  13.1 120.0 all-reduce.2
  238.0 112.0 all-reduce.4
where the time goes:
time: 433 us; the launch traced here: 430 us
  waiting for transfers between devices  161 us (37%)
  other arithmetic  127 us (29%)
  blocking collectives  96 us (22%)
  matrix products  17.4 us (4%)
  between operations  14.1 us (3%)
  local copies, waits for them, and re-layouts  9.33 us (2%)
    psum x2, waiting for transfers between devices, summed_gram(): return lax.psum(products(pair_cols, pair_cols), 'row')  135 us
    psum x1, blocking collectives, body(): sum_squares = lax.psum(jnp.sum(activations * activations), ('pair', 'row'))  96 us
    reduce_sum x64, other arithmetic, masked_diagonal(): return jnp.sum(matrix * mask_table, axis=0)  59.8 us
    add x32, other arithmetic, turn_columns(): upper_part * cos_part + lower_part * sin_part  33 us
    concatenate x32, other arithmetic, roll_lower(): jnp.concatenate((matrix[:, :half_size], jnp.roll(matrix[:, half_size:], o...  26.3 us
    ppermute x1, waiting for transfers between devices, passed_along(): return lax.ppermute(value, axis, pairs)  26.2 us
    dot_general x2, matrix products, products(): return jnp.dot(left_cols.T, right_cols, precision=lax.Precision.HIGHEST)  8.96 us
  transfers between devices with their start and end apart: 3, of which 3 were waited for; matrix products, arithmetic and copies ran while one was open for 0% of the time, Pallas kernels for 0%

commit v1 on v0

v1 whole, which is shorter than its diff:
```python
import jax
import jax.numpy as jnp
from jax import lax
from jax.experimental import pallas as pl
from jax.experimental.pallas import tpu as pltpu
from jax.sharding import PartitionSpec as P

STEPS = 16
BLK = 128
BAND = 16
ROWS = 4 * BAND
TILE = 512
F32 = jnp.float32
BF16 = jnp.bfloat16


def split(value):
    high = value.astype(BF16)
    return high, (value - high.astype(F32)).astype(BF16)


def mm(left, right, dims):
    return lax.dot_general(left, right, (dims, ((), ())), preferred_element_type=F32)


def gram_tile(tile):
    high, low = split(tile)
    rows = ((0,), (0,))
    cross = mm(high, low, rows)
    return mm(high, high, rows) + mm(low, low, rows) + (cross + cross.T)


def take_band(block):
    turned = jnp.concatenate(
        [
            pltpu.roll(block[first : first + 8], (BAND - 8 - first) % BLK, 1)
            for first in range(0, BLK, 8)
        ],
        axis=0,
    )
    left = 7 - lax.broadcasted_iota(jnp.int32, (BLK, BLK), 0) % 8
    for shift in (1, 2, 4):
        turned = jnp.where(left & shift != 0, pltpu.roll(turned, shift, 1), turned)
    return turned.T[:BAND, :]


def store_bands(bands_ref, gram):
    for q in range(4):
        row, col = q // 2 * BLK, q % 2 * BLK
        band = take_band(gram[row : row + BLK, col : col + BLK])
        for k in range(BAND):
            bands_ref[BAND * q + k : BAND * q + k + 1, :] = band[BAND - 1 - k : BAND - k, :]


def put_band(band, first):
    padded = jnp.concatenate((band, jnp.zeros((BLK - BAND, BLK), F32)), axis=0)
    return pltpu.roll(padded.T, first % BLK, 1, stride=1, stride_axis=0)


def half_angle(gap, twice):
    gap_size = jnp.abs(gap)
    twice_size = jnp.abs(twice)
    largest = jnp.maximum(gap_size, twice_size)
    unit = 1.0 / jnp.where(largest > 0.0, largest, 1.0)
    gap_size = jnp.where(largest > 0.0, gap_size * unit, 1.0)
    twice_size = twice_size * unit
    inverse = lax.rsqrt(gap_size * gap_size + twice_size * twice_size)
    half = 0.5 + 0.5 * (gap_size * inverse)
    half_inverse = lax.rsqrt(half)
    large = half * half_inverse
    small = (0.5 * twice_size) * inverse * half_inverse
    sign = jnp.where(twice < 0.0, -1.0, 1.0)
    ahead = gap >= 0.0
    return jnp.where(ahead, large, small), sign * jnp.where(ahead, small, large)


def jacobi_bands(bands):
    last = BAND - 1
    uu, ul, lu, ll = (bands[BAND * i : BAND * (i + 1)] for i in range(4))
    row_ids = lax.broadcasted_iota(jnp.int32, (BAND, BLK), 0)
    is_first = row_ids == 0
    one = jnp.where(row_ids == last, 1.0, 0.0).astype(F32)
    zero = jnp.zeros((BAND, BLK), F32)
    u_top, u_low, l_top, l_low = one, zero, zero, one
    for step in range(STEPS):
        cos_row, sin_row = half_angle(uu[:1, :] - ll[:1, :], 2.0 * ul[:1, :])
        cos_c = jnp.broadcast_to(cos_row, (BAND, BLK))
        sin_c = jnp.broadcast_to(sin_row, (BAND, BLK))
        u_top, l_top = u_top * cos_c + l_top * sin_c, l_top * cos_c - u_top * sin_c
        u_low, l_low = u_low * cos_c + l_low * sin_c, l_low * cos_c - u_low * sin_c
        if step == STEPS - 1:
            break
        cos_d = pltpu.roll(cos_c, 0, 1, stride=1, stride_axis=0)
        sin_d = pltpu.roll(sin_c, 0, 1, stride=1, stride_axis=0)
        uu, lu = uu * cos_c + lu * sin_c, lu * cos_c - uu * sin_c
        ul, ll = ul * cos_c + ll * sin_c, ll * cos_c - ul * sin_c
        uu, ul = uu * cos_d + ul * sin_d, ul * cos_d - uu * sin_d
        lu, ll = lu * cos_d + ll * sin_d, ll * cos_d - lu * sin_d
        ul = pltpu.roll(ul, last, 0)
        lu = jnp.where(is_first, ul, pltpu.roll(pltpu.roll(lu, 1, 0), 1, 1))
        ll = pltpu.roll(ll, 1, 1)
        l_top = pltpu.roll(pltpu.roll(l_top, last, 0), 1, 1)
        l_low = pltpu.roll(pltpu.roll(l_low, last, 0), 1, 1)
    back = BLK - last
    return u_top, u_low, pltpu.roll(l_top, back, 1), pltpu.roll(l_low, back, 1)


def rotation_turned(bands):
    u_top, u_low, l_top, l_low = jacobi_bands(bands)
    upper = jnp.concatenate((put_band(u_top, 1 - BAND), put_band(u_low, 1 - BAND)), axis=1)
    lower = jnp.concatenate((put_band(l_top, 0), put_band(l_low, 0)), axis=1)
    return jnp.concatenate((upper, lower), axis=0)


def times_turned(tile, turned):
    high, low = split(tile)
    turned_high, turned_low = split(turned)
    last = ((1,), (1,))
    return mm(high, turned_high, last) + (mm(high, turned_low, last) + mm(low, turned_high, last))


def gram_kernel(tile_ref, bands_ref, total_ref):
    @pl.when(pl.program_id(0) == 0)
    def _():
        total_ref[...] = jnp.zeros_like(total_ref)

    total_ref[...] += gram_tile(tile_ref[...])

    @pl.when(pl.program_id(0) == pl.num_programs(0) - 1)
    def _():
        store_bands(bands_ref, total_ref[...])


def gram_bands(cols):
    rows = cols.shape[0]
    return pl.pallas_call(
        gram_kernel,
        grid=(rows // TILE,),
        in_specs=[pl.BlockSpec((TILE, 2 * BLK), lambda i: (i, 0))],
        out_specs=pl.BlockSpec((ROWS, BLK), lambda i: (0, 0)),
        out_shape=jax.ShapeDtypeStruct((ROWS, BLK), F32),
        scratch_shapes=[pltpu.VMEM((2 * BLK, 2 * BLK), F32)],
        name="gram_bands",
    )(cols)


def jacobi_kernel(bands_ref, turned_ref):
    bands = bands_ref[0]
    for i in range(1, bands_ref.shape[0]):
        bands = bands + bands_ref[i]
    turned_ref[...] = rotation_turned(bands)


def jacobi(parts):
    return pl.pallas_call(
        jacobi_kernel,
        out_shape=jax.ShapeDtypeStruct((2 * BLK, 2 * BLK), F32),
        name="jacobi",
    )(parts)


def rotate_kernel(tile_ref, turned_ref, out_ref):
    out_ref[...] = times_turned(tile_ref[...], turned_ref[...])


def rotate(cols, turned):
    rows = cols.shape[0]
    return pl.pallas_call(
        rotate_kernel,
        grid=(rows // TILE,),
        in_specs=[
            pl.BlockSpec((TILE, 2 * BLK), lambda i: (i, 0)),
            pl.BlockSpec((2 * BLK, 2 * BLK), lambda i: (0, 0)),
        ],
        out_specs=pl.BlockSpec((TILE, 2 * BLK), lambda i: (i, 0)),
        out_shape=jax.ShapeDtypeStruct(cols.shape, F32),
        name="rotate",
    )(cols, turned)


def passed_along(value, axis, steps):
    count = lax.axis_size(axis)
    pairs = [(source, (source + steps) % count) for source in range(count)]
    return lax.ppermute(value, axis, pairs)


def to_all(value, axis):
    count = lax.axis_size(axis)
    copies = jnp.broadcast_to(value[None], (count,) + value.shape)
    return lax.all_to_all(copies, axis, 0, 0, tiled=True)


def body(activations):
    entry_count = (
        activations.shape[0] * activations.shape[1] * lax.axis_size("pair") * lax.axis_size("row")
    )
    parts_one = lax.all_gather(gram_bands(activations), "row")
    rotated_one = rotate(activations, jacobi(parts_one))
    arrived = passed_along(rotated_one[:, BLK:], "pair", 1)
    diagonals = jnp.sum(parts_one[:, 0] + parts_one[:, 3 * BAND], axis=0)
    diagonals = lax.optimization_barrier((diagonals, rotated_one[:1, :1]))[0]
    sum_squares = jnp.sum(to_all(diagonals.reshape(1, BLK), "pair"))
    rms_value = jnp.sqrt(sum_squares / entry_count)
    pair_two = jnp.concatenate((rotated_one[:, :BLK], arrived), axis=1)
    parts_two = lax.all_gather(gram_bands(pair_two), "row")
    return rotate(pair_two, jacobi(parts_two) / rms_value)


def solution(mesh):
    return jax.shard_map(
        body,
        mesh=mesh,
        in_specs=(P("row", "pair"),),
        out_specs=P("row", "pair"),
        check_vma=False,
    )
```

time: 433 us -> 114 us (0.26)
  waiting for transfers between devices: 161 us -> 0.01 us
  other arithmetic: 127 us -> 4.69 us
  Pallas kernels: 0 us -> 28.3 us
  blocking collectives: 96 us -> 75.1 us
  matrix products: 17.4 us -> 0 us
  between operations: 14.1 us -> 0.72 us
  local copies, waits for them, and re-layouts: 9.33 us -> 1.69 us
    psum x2 -> x0, waiting for transfers between devices: 135 us -> none  [summed_gram(): return lax.psum(products(pair_cols, pair_cols), 'row')]
    psum x1 -> x0, blocking collectives: 96 us -> none  [body(): sum_squares = lax.psum(jnp.sum(activations * activations), ('pair', 'row'))]
    reduce_sum x65 -> x2, other arithmetic: 60.9 us -> 1.51 us  [the longest x1 0.91 us: body(): diagonals = jnp.sum(parts_one[:, 0] + parts_one[:, 3 * BAND], axis=0)]
    all_gather x0 -> x2, blocking collectives: none -> 46 us  [the longest x1 27.6 us: body(): parts_one = lax.all_gather(gram_bands(activations), 'row')]
    add x64 -> x0, other arithmetic: 36.3 us -> none  [the longest x32 33 us: turn_columns(): upper_part * cos_part + lower_part * sin_part]
    all_to_all x0 -> x1, blocking collectives: none -> 29.1 us  [to_all(): return lax.all_to_all(copies, axis, 0, 0, tiled=True)]
    pallas_call x0 -> x6, Pallas kernels: none -> 28.3 us  [the longest x2 9.62 us: jacobi(): pl.pallas_call(jacobi_kernel, out_shape=jax.ShapeDtypeStruct((2 * BLK, 2...]
    ppermute x1, waiting for transfers between devices: 26.2 us -> 0.01 us  [passed_along(): return lax.ppermute(value, axis, pairs)]
  transfers between devices with their start and end apart: 3 -> 1, of which waited for: 3 -> 0; matrix products, arithmetic and copies ran while one was open for 0% -> 1% of each run, Pallas kernels for 0% -> 0%
where the time goes in v1:
time: 114 us
  blocking collectives  75.1 us (66%)
  Pallas kernels  28.3 us (25%)
  other arithmetic  4.69 us (4%)
  starting transfers between devices  3.22 us (3%)
  local copies, waits for them, and re-layouts  1.69 us (1%)
    all_to_all x1, blocking collectives, to_all(): return lax.all_to_all(copies, axis, 0, 0, tiled=True)  29.1 us
    all_gather x1, blocking collectives, body(): parts_one = lax.all_gather(gram_bands(activations), 'row')  27.6 us
    all_gather x1, blocking collectives, body(): parts_two = lax.all_gather(gram_bands(pair_two), 'row')  18.5 us
    pallas_call x2, Pallas kernels, jacobi(): pl.pallas_call(jacobi_kernel, out_shape=jax.ShapeDtypeStruct((2 * BLK, 2...  9.62 us
    pallas_call x2, Pallas kernels, gram_bands(): pl.pallas_call(gram_kernel, grid=(rows // TILE,), in_specs=[pl.BlockSpec(...  9.46 us
    pallas_call x2, Pallas kernels, rotate(): pl.pallas_call(rotate_kernel, grid=(rows // TILE,), in_specs=[pl.BlockSpe...  9.2 us
    ppermute x1, starting transfers between devices, passed_along(): return lax.ppermute(value, axis, pairs)  3.22 us
  transfers between devices with their start and end apart: 1, of which 0 were waited for; matrix products, arithmetic and copies ran while one was open for 1% of the time, Pallas kernels for 0%

profile of v1, /device:TPU:1, one launch (start us, length us, event | category | flops | bytes accessed | tf_op | source)
XLA Modules:
  0.0 113.7 jit_solution(2595727804145714032)
XLA Ops:
  0.0 4.7 %gram_bands.2 = f32[64,128]{1,0:T(8,128)} custom-call(f32[2048,256]{1,0:T(8,128)} %tile_ref.3), custom_call_target="tpu_custom_call" | custom-call | tf_op jit(solution)/shard_map/gram_bands/pallas_call | solution.py:136
  4.7 27.6 %all-gather = f32[1024,128]{1,0:T(8,128)} all-gather(f32[64,128]{1,0:T(8,128)} %gram_bands.2), channel_id=2, replica_groups=mesh['pair'=32,'row'=16] {'row'}, dimensions={0}, use_global_device_ids=true | all-gather | bytes 557056 | tf_op jit(solution)/shard_map/all_gather | solution.py:197
  32.3 4.8 %jacobi.2.turned_ref = f32[256,256]{1,0:T(8,128)} custom-call(f32[16,64,128]{2,1,0:T(8,128)} %bitcast.3), custom_call_target="tpu_custom_call" | custom-call | tf_op jit(solution)/shard_map/jacobi/pallas_call | solution.py:155
  37.1 4.6 %rotate.2 = f32[2048,256]{1,0:T(8,128)} custom-call(f32[2048,256]{1,0:T(8,128)} %tile_ref.3, f32[256,256]{1,0:T(8,128)} %jacobi.2.turned_ref), custom_call_target="tpu_custom_call" | custom-call | tf_op jit(solution)/shard_map/rotate/pallas_call | solution.py:168
  41.7 1.7 %fusion.1 = (f32[2048,128]{1,0:T(8,128)S(1)}, f32[2048,128]{1,0:T(8,128)S(1)}) fusion(f32[2048,256]{1,0:T(8,128)} %rotate.2), kind=kLoop, calls=%fused_computation.4 | loop fusion | bytes 4194304 | tf_op jit(solution)/shard_map/slice | solution.py:204
  43.4 3.2 %collective-permute-start = (f32[2048,128]{1,0:T(8,128)S(1)}, f32[2048,128]{1,0:T(8,128)S(1)}, u32[]{:S(2)}, u32[]{:S(2)}) collective-permute-start(f32[2048,128]{1,0:T(8,128)S(1)} %get-tuple-element.6), channel_id=1, source_target_pairs={{0,16},{16,32},{32,48},{48,64},{64,80},{80,96},{96,112},{112,128},... | collective-permute-start | bytes 3145736 | tf_op jit(solution)/shard_map/ppermute | solution.py:184
  46.6 0.9 fusion
  47.5 29.1 %all_to_all.5 = f32[32,1,128]{2,1,0:T(1,128)S(1)} all-to-all(f32[32,1,128]{2,1,0:T(1,128)S(1)} %broadcast_in_dim.2), channel_id=1, replica_groups=mesh['pair'=32,'row'=16] {'pair'}, dimensions={0} | all-to-all | bytes 32768 | tf_op jit(solution)/shard_map/all_to_all | solution.py:190
  76.6 0.6 reduce_sum.19
  77.9 0.0 collective-permute-done
  77.9 1.5 %pad_maximum_fusion.tile_ref = f32[2048,256]{1,0:T(8,128)} fusion(f32[2048,128]{1,0:T(8,128)S(1)} %collective-permute-done, f32[2048,128]{1,0:T(8,128)S(1)} %get-tuple-element.5), kind=kLoop, calls=%fused_computation | loop fusion | flops 524288 | bytes 4194304 | tf_op jit(solution)/shard_map/concatenate | solution.py:204
  79.4 4.7 %gram_bands.3 = f32[64,128]{1,0:T(8,128)} custom-call(f32[2048,256]{1,0:T(8,128)} %pad_maximum_fusion.tile_ref), custom_call_target="tpu_custom_call" | custom-call | tf_op jit(solution)/shard_map/gram_bands/pallas_call | solution.py:136
  84.1 18.5 %all-gather.1 = f32[1024,128]{1,0:T(8,128)} all-gather(f32[64,128]{1,0:T(8,128)} %gram_bands.3), channel_id=3, replica_groups=mesh['pair'=32,'row'=16] {'row'}, dimensions={0}, use_global_device_ids=true | all-gather | bytes 557056 | tf_op jit(solution)/shard_map/all_gather | solution.py:205
  102.6 4.8 %jacobi.3 = f32[256,256]{1,0:T(8,128)} custom-call(f32[16,64,128]{2,1,0:T(8,128)} %bitcast.5), custom_call_target="tpu_custom_call" | custom-call | tf_op jit(solution)/shard_map/jacobi/pallas_call | solution.py:155
  107.4 1.7 %broadcast_divide_fusion.turned_ref = f32[256,256]{1,0:T(8,128)} fusion(f32[256,256]{1,0:T(8,128)} %jacobi.3, f32[]{:T(128)S(6)} %sqrt.3), kind=kLoop, calls=%fused_computation.1 | loop fusion | flops 65536 | bytes 524292 | tf_op jit(solution)/shard_map/div | solution.py:206
  109.1 4.6 %rotate.3 = f32[2048,256]{1,0:T(8,128)} custom-call(f32[2048,256]{1,0:T(8,128)} %pad_maximum_fusion.tile_ref, f32[256,256]{1,0:T(8,128)} %broadcast_divide_fusion.turned_ref), custom_call_target="tpu_custom_call" | custom-call | tf_op jit(solution)/shard_map/rotate/pallas_call | solution.py:168
  (1 shorter events, 0.0 us)
Async XLA Ops:
  43.4 34.5 %collective-permute-start = (f32[2048,128]{1,0:T(8,128)S(1)}, f32[2048,128]{1,0:T(8,128)S(1)}, u32[]{:S(2)}, u32[]{:S(2)}) collective-permute-start(f32[2048,128]{1,0:T(8,128)S(1)} %get-tuple-element.6), channel_id=1, source_target_pairs={{0,16},{16,32},{32,48},{48,64},{64,80},{80,96},{96,112},{112,128},... | collective-permute-start | bytes 3145736 | tf_op jit(solution)/shard_map/ppermute | solution.py:184

commit v2 on v1

v2 whole, which is shorter than its diff:
```python
import functools

import jax
import jax.numpy as jnp
from jax import lax
from jax.experimental import pallas as pl
from jax.experimental.pallas import tpu as pltpu
from jax.sharding import PartitionSpec as P

STEPS = 16
BLK = 128
BAND = 16
WIDE = 2 * BAND
TILE = 1024
LIMIT = 40 << 20
COST = pl.CostEstimate(flops=2_000_000_000, bytes_accessed=6_000_000, transcendentals=0)
F32 = jnp.float32
BF16 = jnp.bfloat16


def split(value):
    high = value.astype(BF16)
    return high, (value - high.astype(F32)).astype(BF16)


def mm(left, right, dims):
    return lax.dot_general(left, right, (dims, ((), ())), preferred_element_type=F32)


def gram_tile(tile):
    high, low = split(tile)
    rows = ((0,), (0,))
    cross = mm(high, low, rows)
    return mm(high, high, rows) + mm(low, low, rows) + (cross + cross.T)


def take_band(block, width):
    turned = jnp.concatenate(
        [
            pltpu.roll(block[first : first + 8], (width - 8 - first) % BLK, 1)
            for first in range(0, BLK, 8)
        ],
        axis=0,
    )
    left = 7 - lax.broadcasted_iota(jnp.int32, (BLK, BLK), 0) % 8
    for shift in (1, 2, 4):
        turned = jnp.where(left & shift != 0, pltpu.roll(turned, shift, 1), turned)
    return turned.T[:width, :]


def bands_of(block, width):
    band = take_band(block, width)
    return [band[width - 1 - k : width - k, :] for k in range(width)]


def put_band(band, first):
    padded = jnp.concatenate((band, jnp.zeros((BLK - BAND, BLK), F32)), axis=0)
    return pltpu.roll(padded.T, first % BLK, 1, stride=1, stride_axis=0)


def half_angle(gap, twice):
    gap_size = jnp.abs(gap)
    twice_size = jnp.abs(twice)
    largest = jnp.maximum(gap_size, twice_size)
    scale = jnp.where(largest < 2.0**-20, 2.0**80, 1.0)
    gap_size = jnp.where(largest > 0.0, gap_size * scale, 1.0)
    twice_size = twice_size * scale
    inverse = lax.rsqrt(gap_size * gap_size + twice_size * twice_size)
    half = 0.5 + (0.5 * gap_size) * inverse
    half_inverse = lax.rsqrt(half)
    large = half * half_inverse
    small = (0.5 * twice_size) * inverse * half_inverse
    sign = jnp.where(twice < 0.0, -1.0, 1.0)
    ahead = gap >= 0.0
    return jnp.where(ahead, large, small), sign * jnp.where(ahead, small, large)


def row_copies(rows, index):
    return jnp.broadcast_to(rows[index : index + 1, :], (8, BLK))


def ahead_by_one(rows):
    return pltpu.roll(rows, 1, 1)


def jacobi_bands(uu, ul, lu, ll):
    count = uu.shape[0]
    last = BAND - 1
    is_first = lax.broadcasted_iota(jnp.int32, (count, BLK), 0) == 0
    row_ids = lax.broadcasted_iota(jnp.int32, (BAND, BLK), 0)
    one = jnp.where(row_ids == last, 1.0, 0.0).astype(F32)
    zero = jnp.zeros((BAND, BLK), F32)
    u_top, u_low, l_top, l_low = one, zero, zero, one
    u_diag, l_diag, coupling = row_copies(uu, 0), row_copies(ll, 0), row_copies(ul, 0)
    for step in range(STEPS):
        cos, sin = half_angle(u_diag - l_diag, 2.0 * coupling)
        final_step = step == STEPS - 1
        if not final_step:
            u_past, l_past, x_past = (ahead_by_one(v) for v in (u_diag, l_diag, coupling))
            cos_past, sin_past = ahead_by_one(cos), ahead_by_one(sin)
            u_diag, coupling = (
                cos * (cos * u_diag + sin * coupling) + sin * (cos * coupling + sin * l_diag),
                cos_past * (cos * row_copies(ul, 1) + sin * row_copies(ll, 1))
                - sin_past * (cos * row_copies(uu, 1) + sin * row_copies(lu, 1)),
            )
            l_diag = cos_past * (cos_past * l_past - sin_past * x_past) - sin_past * (
                cos_past * x_past - sin_past * u_past
            )
        cos_b = jnp.concatenate([cos] * (BAND // 8), axis=0)
        sin_b = jnp.concatenate([sin] * (BAND // 8), axis=0)
        u_top, l_top = u_top * cos_b + l_top * sin_b, l_top * cos_b - u_top * sin_b
        u_low, l_low = u_low * cos_b + l_low * sin_b, l_low * cos_b - u_low * sin_b
        if final_step and count == BAND:
            break
        cos_c = jnp.concatenate([cos] * (count // 8), axis=0)
        sin_c = jnp.concatenate([sin] * (count // 8), axis=0)
        cos_d = jnp.concatenate(
            [pltpu.roll(cos, 8 * i, 1, stride=1, stride_axis=0) for i in range(count // 8)], axis=0
        )
        sin_d = jnp.concatenate(
            [pltpu.roll(sin, 8 * i, 1, stride=1, stride_axis=0) for i in range(count // 8)], axis=0
        )
        uu, lu = uu * cos_c + lu * sin_c, lu * cos_c - uu * sin_c
        ul, ll = ul * cos_c + ll * sin_c, ll * cos_c - ul * sin_c
        uu, ul = uu * cos_d + ul * sin_d, ul * cos_d - uu * sin_d
        lu, ll = lu * cos_d + ll * sin_d, ll * cos_d - lu * sin_d
        if final_step:
            break
        ul = pltpu.roll(ul, count - 1, 0)
        lu = jnp.where(is_first, ul, ahead_by_one(pltpu.roll(lu, 1, 0)))
        ll = ahead_by_one(ll)
        l_top = ahead_by_one(pltpu.roll(l_top, last, 0))
        l_low = ahead_by_one(pltpu.roll(l_low, last, 0))
    back = BLK - last
    l_top, l_low = pltpu.roll(l_top, back, 1), pltpu.roll(l_low, back, 1)
    return u_top, u_low, l_top, l_low, uu[:BAND], pltpu.roll(ll[:BAND], back, 1)


def turned_half(top, low, first):
    return jnp.concatenate((put_band(top, first), put_band(low, first)), axis=1)


def times_turned(tile, turned):
    high, low = split(tile)
    turned_high, turned_low = split(turned)
    last = ((1,), (1,))
    return mm(high, turned_high, last) + (mm(high, turned_low, last) + mm(low, turned_high, last))


def summed(parts_ref, first=0, step=1):
    total = parts_ref[first]
    for i in range(first + step, parts_ref.shape[0], step):
        total = total + parts_ref[i]
    return total


def jacobi_kernel(core_ref, parts_ref, turned_ref, sent_ref, kept_ref):
    upper, lower = summed(parts_ref, 0, 2), summed(parts_ref, 1, 2)
    u_top, u_low, l_top, l_low, uu, ll = jacobi_bands(
        upper[:WIDE], upper[WIDE:], lower[:WIDE], lower[WIDE:]
    )
    first_core = core_ref[0] == 0
    sent_ref[:BAND, :] = jnp.where(first_core, l_top, u_top)
    sent_ref[BAND : 2 * BAND, :] = jnp.where(first_core, l_low, u_low)
    sent_ref[2 * BAND :, :] = jnp.where(first_core, ll, uu)
    kept_ref[...] = jnp.where(first_core, uu, ll)
    turned_ref[:BLK, :] = turned_half(u_top, u_low, 1 - BAND)
    turned_ref[BLK:, :] = turned_half(l_top, l_low, 0)


def jacobi(core, parts):
    return pl.pallas_call(
        jacobi_kernel,
        in_specs=[
            pl.BlockSpec(memory_space=pltpu.SMEM),
            pl.BlockSpec(memory_space=pltpu.VMEM),
        ],
        out_shape=(
            jax.ShapeDtypeStruct((2 * BLK, 2 * BLK), F32),
            jax.ShapeDtypeStruct((3 * BAND, BLK), F32),
            jax.ShapeDtypeStruct((BAND, BLK), F32),
        ),
        name="jacobi",
    )(core, parts)


def rotate_kernel(tile_ref, turned_ref, upper_ref, lower_ref):
    out = times_turned(tile_ref[...], turned_ref[...])
    upper_ref[...] = out[:, :BLK]
    lower_ref[...] = out[:, BLK:]


def rotate(cols, turned):
    rows = cols.shape[0]
    half = jax.ShapeDtypeStruct((rows, BLK), F32)
    half_spec = pl.BlockSpec((TILE, BLK), lambda i: (i, 0))
    return pl.pallas_call(
        rotate_kernel,
        grid=(rows // TILE,),
        in_specs=[
            pl.BlockSpec((TILE, 2 * BLK), lambda i: (i, 0)),
            pl.BlockSpec((2 * BLK, 2 * BLK), lambda i: (0, 0)),
        ],
        out_specs=(half_spec, half_spec),
        out_shape=(half, half),
        compiler_params=pltpu.CompilerParams(vmem_limit_bytes=LIMIT),
        cost_estimate=COST,
        name="rotate",
    )(cols, turned)


def cross_tile(left, right):
    left_high, left_low = split(left)
    right_high, right_low = split(right)
    rows = ((0,), (0,))
    return (
        mm(left_high, right_high, rows)
        + mm(left_low, right_low, rows)
        + (mm(left_high, right_low, rows) + mm(left_low, right_high, rows))
    )


def link_kernel(
    core_ref, raw_ref, got_ref, kept_ref, traces_ref, upper_ref, lower_ref,
    other_ref, bands_ref, diag_ref, turned_ref, total_ref,
):
    first_core = core_ref[0] == 0

    @pl.when(pl.program_id(0) == 0)
    def _():
        got = got_ref[...]
        top, low = got[:BAND], got[BAND : 2 * BAND]

        @pl.when(first_core)
        def _():
            turned_ref[...] = turned_half(top, low, 0)
            diag_ref[:BAND, :] = kept_ref[...]
            diag_ref[BAND:, :] = got[2 * BAND :]

        @pl.when(jnp.logical_not(first_core))
        def _():
            turned_ref[...] = turned_half(top, low, 1 - BAND)
            diag_ref[:BAND, :] = got[2 * BAND :]
            diag_ref[BAND:, :] = kept_ref[...]

        total_ref[...] = jnp.zeros_like(total_ref)

    other = times_turned(raw_ref[...], turned_ref[...])
    other_ref[...] = other
    left = jnp.where(first_core, upper_ref[...], other)
    right = jnp.where(first_core, other, lower_ref[...])
    total_ref[...] += cross_tile(left, right)

    @pl.when(pl.program_id(0) == pl.num_programs(0) - 1)
    def _():
        cross = total_ref[...]
        bands = jnp.concatenate(
            bands_of(cross, BAND) + [summed(traces_ref)] + bands_of(cross.T, BAND)[1:], axis=0
        )
        for i in range(bands_ref.shape[0]):
            bands_ref[i] = bands


def link(core, raw, got, kept, traces, upper, lower, copies):
    rows = raw.shape[0]
    half_spec = pl.BlockSpec((TILE, BLK), lambda i: (i, 0))
    return pl.pallas_call(
        link_kernel,
        grid=(rows // TILE,),
        in_specs=[
            pl.BlockSpec(memory_space=pltpu.SMEM),
            pl.BlockSpec((TILE, 2 * BLK), lambda i: (i, 0)),
            pl.BlockSpec((3 * BAND, BLK), lambda i: (0, 0)),
            pl.BlockSpec((BAND, BLK), lambda i: (0, 0)),
            pl.BlockSpec(traces.shape, lambda i: (0, 0, 0)),
            half_spec,
            half_spec,
        ],
        out_specs=(
            half_spec,
            pl.BlockSpec((copies, 2 * BAND, BLK), lambda i: (0, 0, 0)),
            pl.BlockSpec((2 * BAND, BLK), lambda i: (0, 0)),
        ),
        out_shape=(
            jax.ShapeDtypeStruct((rows, BLK), F32),
            jax.ShapeDtypeStruct((copies, 2 * BAND, BLK), F32),
            jax.ShapeDtypeStruct((2 * BAND, BLK), F32),
        ),
        scratch_shapes=[pltpu.VMEM((BLK, 2 * BLK), F32), pltpu.VMEM((BLK, BLK), F32)],
        compiler_params=pltpu.CompilerParams(vmem_limit_bytes=LIMIT),
        name="link",
    )(core, raw, got, kept, traces, upper, lower)


def final_kernel(
    entry_count, core_ref, bands_ref, upper_ref, other_ref, came_ref, out_ref, turned_ref
):
    @pl.when(pl.program_id(0) == 0)
    def _():
        ul, lu, uu, ll = (bands_ref[BAND * i : BAND * (i + 1), :] for i in range(4))
        rms = jnp.sqrt(jnp.sum(lu[:1], axis=1, keepdims=True) / entry_count)
        lu = jnp.concatenate((ul[:1], lu[1:]), axis=0)
        u_top, u_low, l_top, l_low, _, _ = jacobi_bands(uu, ul, lu, ll)
        turned_ref[:BLK, :] = turned_half(u_top, u_low, 1 - BAND) / rms
        turned_ref[BLK:, :] = turned_half(l_top, l_low, 0) / rms

    lower = jnp.where(core_ref[0] == 0, other_ref[...], came_ref[...])
    pair = jnp.concatenate((upper_ref[...], lower), axis=1)
    out_ref[...] = times_turned(pair, turned_ref[...])


def final(entry_count, core, bands, upper, other, came):
    rows = upper.shape[0]
    half_spec = pl.BlockSpec((TILE, BLK), lambda i: (i, 0))
    return pl.pallas_call(
        functools.partial(final_kernel, entry_count),
        grid=(rows // TILE,),
        in_specs=[
            pl.BlockSpec(memory_space=pltpu.SMEM),
            pl.BlockSpec((4 * BAND, BLK), lambda i: (0, 0)),
            half_spec,
            half_spec,
            half_spec,
        ],
        out_specs=pl.BlockSpec((TILE, 2 * BLK), lambda i: (i, 0)),
        out_shape=jax.ShapeDtypeStruct((rows, 2 * BLK), F32),
        scratch_shapes=[pltpu.VMEM((2 * BLK, 2 * BLK), F32)],
        compiler_params=pltpu.CompilerParams(vmem_limit_bytes=LIMIT),
        name="final",
    )(core, bands, upper, other, came)


def gram_kernel(core_ref, tile_ref, bands_ref, trace_ref, total_ref):
    @pl.when(pl.program_id(0) == 0)
    def _():
        total_ref[...] = jnp.zeros_like(total_ref)

    total_ref[...] += gram_tile(tile_ref[...])

    @pl.when(pl.program_id(0) == pl.num_programs(0) - 1)
    def _():
        gram = total_ref[...]
        halves = []
        for row in (0, BLK):
            upper = bands_of(gram[row : row + BLK, :BLK], WIDE)
            lower = bands_of(gram[row : row + BLK, BLK:], WIDE)
            halves.append(jnp.concatenate(upper + lower, axis=0))
        core = core_ref[0]
        bands_ref[core] = halves[0]
        bands_ref[1 - core] = halves[1]
        trace_ref[...] = jnp.broadcast_to(
            (halves[0][:1] + halves[1][WIDE : WIDE + 1])[None], trace_ref.shape
        )


def gram_bands(core, cols, copies):
    rows = cols.shape[0]
    return pl.pallas_call(
        gram_kernel,
        grid=(rows // TILE,),
        in_specs=[
            pl.BlockSpec(memory_space=pltpu.SMEM),
            pl.BlockSpec((TILE, 2 * BLK), lambda i: (i, 0)),
        ],
        out_specs=(
            pl.BlockSpec((2, 2 * WIDE, BLK), lambda i: (0, 0, 0)),
            pl.BlockSpec((copies, 1, BLK), lambda i: (0, 0, 0)),
        ),
        out_shape=(
            jax.ShapeDtypeStruct((2, 2 * WIDE, BLK), F32),
            jax.ShapeDtypeStruct((copies, 1, BLK), F32),
        ),
        scratch_shapes=[pltpu.VMEM((2 * BLK, 2 * BLK), F32)],
        compiler_params=pltpu.CompilerParams(vmem_limit_bytes=LIMIT),
        name="gram_bands",
    )(core, cols)


class Ring:
    def __init__(self, pairs, rows):
        self.pairs, self.rows = pairs, rows

    def at(self, pair, row):
        return pair % self.pairs * self.rows + row

    def moves(self, cores, steps):
        return [
            (self.at(pair, row), self.at(pair + steps, row))
            for pair in range(self.pairs)
            for row in range(self.rows)
            if row % 2 in cores
        ]

    def swapped(self):
        return self.moves((0,), 1) + self.moves((1,), -1)

    def to_second_core(self):
        return [
            (self.at(pair, row), self.at(pair, row + 1))
            for pair in range(self.pairs)
            for row in range(0, self.rows, 2)
        ]

    def to_other_core(self):
        return [(at, at ^ 1) for at in range(self.pairs * self.rows)]

    def links(self):
        return [
            [self.at(pair, row) for row in range(0, self.rows, 2)]
            + [self.at(pair - 1, row) for row in range(1, self.rows, 2)]
            for pair in range(self.pairs)
        ]


AXES = ("pair", "row")


def body(activations):
    pairs, rows = lax.axis_size("pair"), lax.axis_size("row")
    ring = Ring(pairs, rows)
    entry_count = activations.shape[0] * activations.shape[1] * pairs * rows
    core = (lax.axis_index("row") % 2).astype(jnp.int32).reshape(1)

    raw = lax.ppermute(activations, AXES, ring.swapped())
    bands, traces = gram_bands(core, activations, pairs)
    traces = lax.all_to_all(traces, "pair", 0, 0, tiled=True)
    bands = bands[0] + lax.ppermute(bands[1], AXES, ring.to_other_core())
    turned, sent, kept = jacobi(core, lax.all_gather(bands, "row"))
    got = lax.ppermute(sent, AXES, ring.swapped())
    upper, lower = rotate(activations, turned)
    other, bands, diag = link(core, raw, got, kept, traces, upper, lower, rows)
    lower, bands = lax.optimization_barrier((lower, bands))
    came = lax.ppermute(lower, AXES, ring.moves((1,), 1))
    parts = lax.all_to_all(bands, AXES, 0, 0, axis_index_groups=ring.links(), tiled=True)
    bands = jnp.concatenate((jnp.sum(parts, axis=0), diag), axis=0)
    arrived = lax.ppermute(bands, AXES, ring.to_second_core())
    bands = jnp.where(core[0] == 0, bands, arrived)
    return final(float(entry_count), core, bands, upper, other, came)


def solution(mesh):
    return jax.shard_map(
        body,
        mesh=mesh,
        in_specs=(P("row", "pair"),),
        out_specs=P("row", "pair"),
        check_vma=False,
    )
```

time: 114 us -> 92.4 us (0.81)
  blocking collectives: 75.1 us -> 37.7 us
  starting transfers between devices: 3.22 us -> 27.4 us
  Pallas kernels: 28.3 us -> 17.5 us
  waiting for transfers between devices: 0.01 us -> 6.59 us
  other arithmetic: 4.69 us -> 0.04 us
    all_gather x2 -> x1, blocking collectives: 46 us -> 24.4 us  [body(): turned, sent, kept = jacobi(core, lax.all_gather(bands, 'row'))]
    ppermute x1 -> x5, starting transfers between devices: 3.22 us -> 20.7 us  [the longest x1 8.11 us: body(): raw = lax.ppermute(activations, AXES, ring.swapped())]
    all_to_all x1, blocking collectives: 29.1 us -> 13.3 us  [body(): lax.all_to_all(bands, AXES, 0, 0, axis_index_groups=ring.links(), tiled=T...]
    pallas_call x2 -> x1, Pallas kernels: 9.2 us -> 2.03 us  [rotate(): pl.pallas_call(rotate_kernel, grid=(rows // TILE,), in_specs=[pl.BlockSpe...]
    pallas_call x2 -> x1, Pallas kernels: 9.46 us -> 2.6 us  [gram_bands(): pl.pallas_call(gram_kernel, grid=(rows // TILE,), in_specs=[pl.BlockSpec(...]
    all_to_all x0 -> x1, starting transfers between devices: none -> 6.73 us  [body(): traces = lax.all_to_all(traces, 'pair', 0, 0, tiled=True)]
    ppermute x1 -> x5, waiting for transfers between devices: 0.01 us -> 6.59 us  [the longest x1 6.58 us: body(): arrived = lax.ppermute(bands, AXES, ring.to_second_core())]
    pallas_call x2 -> x3, Pallas kernels: 9.62 us -> 12.9 us  [the longest x1 4.95 us: link(): pl.pallas_call(link_kernel, grid=(rows // TILE,), in_specs=[pl.BlockSpec(...]
  transfers between devices with their start and end apart: 1 -> 6, of which waited for: 0 -> 1; matrix products, arithmetic and copies ran while one was open for 1% -> 0% of each run, Pallas kernels for 0% -> 9%
where the time goes in v2:
time: 92.4 us; the launch traced here: 92 us
  blocking collectives  37.7 us (41%)
  starting transfers between devices  27.4 us (30%)
  Pallas kernels  17.5 us (19%)
  waiting for transfers between devices  6.59 us (7%)
  local copies, waits for them, and re-layouts  2.54 us (3%)
    all_gather x1, blocking collectives, body(): turned, sent, kept = jacobi(core, lax.all_gather(bands, 'row'))  24.4 us
    all_to_all x1, blocking collectives, body(): lax.all_to_all(bands, AXES, 0, 0, axis_index_groups=ring.links(), tiled=T...  13.3 us
    ppermute x1, starting transfers between devices, body(): raw = lax.ppermute(activations, AXES, ring.swapped())  8.11 us
    ppermute x1, starting transfers between devices, body(): got = lax.ppermute(sent, AXES, ring.swapped())  6.82 us
    all_to_all x1, starting transfers between devices, body(): traces = lax.all_to_all(traces, 'pair', 0, 0, tiled=True)  6.73 us
    ppermute x1, waiting for transfers between devices, body(): arrived = lax.ppermute(bands, AXES, ring.to_second_core())  6.58 us
    pallas_call x1, Pallas kernels, link(): pl.pallas_call(link_kernel, grid=(rows // TILE,), in_specs=[pl.BlockSpec(...  4.95 us
    pallas_call x1, Pallas kernels, final(): pl.pallas_call(functools.partial(final_kernel, entry_count), grid=(rows /...  4.2 us
  transfers between devices with their start and end apart: 6, of which 1 were waited for; matrix products, arithmetic and copies ran while one was open for 0% of the time, Pallas kernels for 9%

profile of v2, /device:TPU:1, one launch (start us, length us, event | category | flops | bytes accessed | tf_op | source)
XLA Modules:
  0.0 92.0 jit_solution(7010144125485587593)
XLA Ops:
  0.0 8.1 %collective-permute-start.1 = (f32[2048,256]{1,0:T(8,128)}, f32[2048,256]{1,0:T(8,128)}, u32[]{:S(2)}, u32[]{:S(2)}) collective-permute-start(f32[2048,256]{1,0:T(8,128)} %tile_ref.3), channel_id=1, source_target_pairs={{0,16},{2,18},{4,20},{6,22},{8,24},{10,26},{12,28},{14,30},{16,32}... | collective-permute-start | bytes 6291464 | tf_op jit(solution)/shard_map/ppermute | solution.py:424
  8.1 0.0 copy-start
  8.1 1.6 %copy-done = f32[2048,256]{1,0:T(8,128)S(1)} copy-done((f32[2048,256]{1,0:T(8,128)S(1)}, f32[2048,256]{1,0:T(8,128)}, u32[]{:S(2)}) %copy-start) | copy-done | bytes 2097176
  9.7 0.0 copy-start.1
  9.7 2.6 %gram_bands.1 = (f32[2,64,128]{2,1,0:T(8,128)S(1)}, f32[32,1,128]{2,1,0:T(1,128)}) custom-call(s32[1]{0:T(128)} %bitcast.core_ref, f32[2048,256]{1,0:T(8,128)S(1)} %copy-done), custom_call_target="tpu_custom_call" | custom-call | tf_op jit(solution)/shard_map/gram_bands/pallas_call | solution.py:358
  12.3 2.6 %collective-permute-start = (f32[64,128]{1,0:T(8,128)S(1)}, f32[64,128]{1,0:T(8,128)S(1)}, u32[]{:S(2)}, u32[]{:S(2)}) collective-permute-start(f32[64,128]{1,0:T(8,128)S(1)} %slice_bitcast_fusion), channel_id=1, source_target_pairs={{0,1},{1,0},{2,3},{3,2},{4,5},{5,4},{6,7},{7,6},{8,9},{9,8},{10,11... | collective-permute-start | bytes 98312 | tf_op jit(solution)/shard_map/ppermute | solution.py:427
  14.9 6.7 %all-to-all-start = ((f32[32,1,128]{2,1,0:T(1,128)}), f32[32,1,128]{2,1,0:T(1,128)S(1)}, u32[]{:S(2)}, u32[]{:S(2)}) async-start(f32[32,1,128]{2,1,0:T(1,128)} %get-tuple-element.22), calls=%async_computation | async-start | bytes 32768 | tf_op jit(solution)/shard_map/all_to_all | solution.py:426
  21.7 0.0 collective-permute-done
  21.7 24.4 %all-gather = f32[1024,128]{1,0:T(8,128)} all-gather(f32[64,128]{1,0:T(8,128)S(1)} %bitcast_add_fusion), channel_id=2, replica_groups=mesh['pair'=32,'row'=16] {'row'}, dimensions={0}, use_global_device_ids=true | all-gather | bytes 557056 | tf_op jit(solution)/shard_map/all_gather | solution.py:428
  46.0 3.8 %jacobi.1 = (f32[256,256]{1,0:T(8,128)}, f32[48,128]{1,0:T(8,128)}, f32[16,128]{1,0:T(8,128)}) custom-call(s32[1]{0:T(128)} %bitcast.core_ref, f32[16,64,128]{2,1,0:T(8,128)} %bitcast.6), custom_call_target="tpu_custom_call" | custom-call | tf_op jit(solution)/shard_map/jacobi/pallas_call | solution.py:172
  49.8 6.8 %collective-permute-start.2 = (f32[48,128]{1,0:T(8,128)}, f32[48,128]{1,0:T(8,128)S(1)}, u32[]{:S(2)}, u32[]{:S(2)}) collective-permute-start(f32[48,128]{1,0:T(8,128)} %get-tuple-element.20), channel_id=1, source_target_pairs={{0,16},{2,18},{4,20},{6,22},{8,24},{10,26},{12,28},{14,30},{16,32}... | collective-permute-start | bytes 73736 | tf_op jit(solution)/shard_map/ppermute | solution.py:429
  56.6 0.0 copy-done.1
  56.6 0.0 copy-start.3
  56.6 0.9 %copy-done.3 = f32[256,256]{1,0:T(8,128)S(1)} copy-done((f32[256,256]{1,0:T(8,128)S(1)}, f32[256,256]{1,0:T(8,128)}, u32[]{:S(2)}) %copy-start.3) | copy-done | bytes 262168
  57.6 0.0 copy-start.2
  57.6 2.0 %rotate.1 = (f32[2048,128]{1,0:T(8,128)S(1)}, f32[2048,128]{1,0:T(8,128)}) custom-call(f32[2048,256]{1,0:T(8,128)S(1)} %copy-done.1, f32[256,256]{1,0:T(8,128)S(1)} %copy-done.3), custom_call_target="tpu_custom_call" | custom-call | flops 2000000000 | bytes 6000000 | tf_op jit(solution)/shard_map/rotate/pallas_call | solution.py:197
  59.6 0.0 all-to-all-done.traces_ref
  59.6 0.0 collective-permute-done.2.got_ref
  59.6 0.0 collective-permute-done.1.raw_ref
  59.6 0.0 copy-done.2
  59.6 4.9 %link.1 = (f32[2048,128]{1,0:T(8,128)S(1)}, f32[16,32,128]{2,1,0:T(8,128)S(1)}, f32[32,128]{1,0:T(8,128)S(1)}) custom-call(s32[1]{0:T(128)} %bitcast.core_ref, f32[2048,256]{1,0:T(8,128)} %collective-permute-done.1.raw_ref, f32[48,128]{1,0:T(8,128)S(1)} %collective-permute-done.2.got_ref, f32[16,128]{1,0:T(8,128)S(1)} %copy-done.2, ...), custom_call_target="tpu_custom_call" | custom-call | tf_op jit(solution)/shard_map/link/pallas_call | solution.py:267
  64.6 1.9 %collective-permute-start.4 = (f32[2048,128]{1,0:T(8,128)}, f32[2048,128]{1,0:T(8,128)S(1)}, u32[]{:S(2)}, u32[]{:S(2)}) collective-permute-start(f32[2048,128]{1,0:T(8,128)} %get-tuple-element.28.lower_ref), channel_id=1, source_target_pairs={{1,17},{3,19},{5,21},{7,23},{9,25},{11,27},{13,29},{15,31},{17,33}... | collective-permute-start | bytes 3145736 | tf_op jit(solution)/shard_map/ppermute | solution.py:433
  66.5 13.3 %all_to_all.10 = f32[16,32,128]{2,1,0:T(8,128)S(1)} all-to-all(f32[16,32,128]{2,1,0:T(8,128)S(1)} %get-tuple-element.25), channel_id=1, replica_groups={{0,2,4,6,8,10,12,14,497,499,501,503,505,507,509,511},{16,18,20,22,24,26..., dimensions={0} | all-to-all | bytes 524288 | tf_op jit(solution)/shard_map/all_to_all | solution.py:434
  79.9 1.3 %collective-permute-start.3 = (f32[64,128]{1,0:T(8,128)S(1)}, f32[64,128]{1,0:T(8,128)S(1)}, u32[]{:S(2)}, u32[]{:S(2)}) collective-permute-start(f32[64,128]{1,0:T(8,128)S(1)} %pad_maximum_fusion), channel_id=1, source_target_pairs={{0,1},{2,3},{4,5},{6,7},{8,9},{10,11},{12,13},{14,15},{16,17},{18,... | collective-permute-start | bytes 98312 | tf_op jit(solution)/shard_map/ppermute | solution.py:436
  81.2 6.6 %collective-permute-done.3 = f32[64,128]{1,0:T(8,128)S(1)} collective-permute-done((f32[64,128]{1,0:T(8,128)S(1)}, f32[64,128]{1,0:T(8,128)S(1)}, u32[]{:S(2)}, u32[]{:S(2)}) %collective-permute-start.3) | collective-permute-done | bytes 32800 | tf_op jit(solution)/shard_map/ppermute | solution.py:436
  87.8 0.0 collective-permute-done.4.came_ref
  87.8 4.2 %final.1 = f32[2048,256]{1,0:T(8,128)} custom-call(s32[1]{0:T(128)} %bitcast.core_ref, f32[64,128]{1,0:T(8,128)S(1)} %broadcast_select_fusion.bands_ref, f32[2048,128]{1,0:T(8,128)S(1)} %get-tuple-element.23.upper_ref, f32[2048,128]{1,0:T(8,128)S(1)} %get-tuple-element.27.other_ref, f32[2048,128]{1,0:T(8,128)S(1)} %collective-permute-done.4.came_ref), custom_call_target="tpu_custom_call" | custom-call | tf_op jit(solution)/shard_map/final/pallas_call | solution.py:315
  (5 shorter events, 0.0 us)
Async XLA Ops:
  0.0 59.6 %collective-permute-start.1 = (f32[2048,256]{1,0:T(8,128)}, f32[2048,256]{1,0:T(8,128)}, u32[]{:S(2)}, u32[]{:S(2)}) collective-permute-start(f32[2048,256]{1,0:T(8,128)} %tile_ref.3), channel_id=1, source_target_pairs={{0,16},{2,18},{4,20},{6,22},{8,24},{10,26},{12,28},{14,30},{16,32}... | collective-permute-start | bytes 6291464 | tf_op jit(solution)/shard_map/ppermute | solution.py:424
  8.1 1.6 %copy-start = (f32[2048,256]{1,0:T(8,128)S(1)}, f32[2048,256]{1,0:T(8,128)}, u32[]{:S(2)}) copy-start(f32[2048,256]{1,0:T(8,128)} %tile_ref.3) | copy-start | bytes 6291460
  9.7 46.9 %copy-start.1 = (f32[2048,256]{1,0:T(8,128)S(1)}, f32[2048,256]{1,0:T(8,128)}, u32[]{:S(2)}) copy-start(f32[2048,256]{1,0:T(8,128)} %tile_ref.3) | copy-start | bytes 6291460
  12.3 9.3 %collective-permute-start = (f32[64,128]{1,0:T(8,128)S(1)}, f32[64,128]{1,0:T(8,128)S(1)}, u32[]{:S(2)}, u32[]{:S(2)}) collective-permute-start(f32[64,128]{1,0:T(8,128)S(1)} %slice_bitcast_fusion), channel_id=1, source_target_pairs={{0,1},{1,0},{2,3},{3,2},{4,5},{5,4},{6,7},{7,6},{8,9},{9,8},{10,11... | collective-permute-start | bytes 98312 | tf_op jit(solution)/shard_map/ppermute | solution.py:427
  14.9 44.7 %all-to-all-start = ((f32[32,1,128]{2,1,0:T(1,128)}), f32[32,1,128]{2,1,0:T(1,128)S(1)}, u32[]{:S(2)}, u32[]{:S(2)}) async-start(f32[32,1,128]{2,1,0:T(1,128)} %get-tuple-element.22), calls=%async_computation | async-start | bytes 32768 | tf_op jit(solution)/shard_map/all_to_all | solution.py:426
  49.8 9.8 %collective-permute-start.2 = (f32[48,128]{1,0:T(8,128)}, f32[48,128]{1,0:T(8,128)S(1)}, u32[]{:S(2)}, u32[]{:S(2)}) collective-permute-start(f32[48,128]{1,0:T(8,128)} %get-tuple-element.20), channel_id=1, source_target_pairs={{0,16},{2,18},{4,20},{6,22},{8,24},{10,26},{12,28},{14,30},{16,32}... | collective-permute-start | bytes 73736 | tf_op jit(solution)/shard_map/ppermute | solution.py:429
  56.6 1.0 %copy-start.3 = (f32[256,256]{1,0:T(8,128)S(1)}, f32[256,256]{1,0:T(8,128)}, u32[]{:S(2)}) copy-start(f32[256,256]{1,0:T(8,128)} %get-tuple-element.18.turned_ref) | copy-start | bytes 786436
  57.6 2.1 %copy-start.2 = (f32[16,128]{1,0:T(8,128)S(1)}, f32[16,128]{1,0:T(8,128)}, u32[]{:S(2)}) copy-start(f32[16,128]{1,0:T(8,128)} %get-tuple-element.21.kept_ref) | copy-start | bytes 24580
  64.6 23.2 %collective-permute-start.4 = (f32[2048,128]{1,0:T(8,128)}, f32[2048,128]{1,0:T(8,128)S(1)}, u32[]{:S(2)}, u32[]{:S(2)}) collective-permute-start(f32[2048,128]{1,0:T(8,128)} %get-tuple-element.28.lower_ref), channel_id=1, source_target_pairs={{1,17},{3,19},{5,21},{7,23},{9,25},{11,27},{13,29},{15,31},{17,33}... | collective-permute-start | bytes 3145736 | tf_op jit(solution)/shard_map/ppermute | solution.py:433
  79.9 7.9 %collective-permute-start.3 = (f32[64,128]{1,0:T(8,128)S(1)}, f32[64,128]{1,0:T(8,128)S(1)}, u32[]{:S(2)}, u32[]{:S(2)}) collective-permute-start(f32[64,128]{1,0:T(8,128)S(1)} %pad_maximum_fusion), channel_id=1, source_target_pairs={{0,1},{2,3},{4,5},{6,7},{8,9},{10,11},{12,13},{14,15},{16,17},{18,... | collective-permute-start | bytes 98312 | tf_op jit(solution)/shard_map/ppermute | solution.py:436

commit v3 on v1

v3 whole, which is shorter than its diff:
```python
import functools

import jax
import jax.numpy as jnp
from jax import lax
from jax.experimental import pallas as pl
from jax.experimental.pallas import tpu as pltpu
from jax.sharding import PartitionSpec as P

STEPS = 16
BLK = 128
BAND = 16
ROWS = 4 * BAND
TILE = 1024
EARLY = 1216
LIMIT = 24 << 20
COST = pl.CostEstimate(flops=2_000_000_000, bytes_accessed=6_000_000, transcendentals=0)
F32 = jnp.float32
BF16 = jnp.bfloat16


def split(value):
    high = value.astype(BF16)
    return high, (value - high.astype(F32)).astype(BF16)


def mm(left, right, dims):
    return lax.dot_general(left, right, (dims, ((), ())), preferred_element_type=F32)


def gram_tile(tile):
    high, low = split(tile)
    rows = ((0,), (0,))
    cross = mm(high, low, rows)
    return mm(high, high, rows) + mm(low, low, rows) + (cross + cross.T)


def take_band(block, width):
    turned = jnp.concatenate(
        [
            pltpu.roll(block[first : first + 8], (width - 8 - first) % BLK, 1)
            for first in range(0, BLK, 8)
        ],
        axis=0,
    )
    left = 7 - lax.broadcasted_iota(jnp.int32, (BLK, BLK), 0) % 8
    for shift in (1, 2, 4):
        turned = jnp.where(left & shift != 0, pltpu.roll(turned, shift, 1), turned)
    return turned.T[:width, :]


def bands_of(block, width):
    band = take_band(block, width)
    return [band[width - 1 - k : width - k, :] for k in range(width)]


def put_band(band, first):
    padded = jnp.concatenate((band, jnp.zeros((BLK - BAND, BLK), F32)), axis=0)
    return pltpu.roll(padded.T, first % BLK, 1, stride=1, stride_axis=0)


def half_angle(gap, twice):
    gap_size = jnp.abs(gap)
    twice_size = jnp.abs(twice)
    largest = jnp.maximum(gap_size, twice_size)
    scale = jnp.where(largest < 2.0**-20, 2.0**80, 1.0)
    gap_size = jnp.where(largest > 0.0, gap_size * scale, 1.0)
    twice_size = twice_size * scale
    inverse = lax.rsqrt(gap_size * gap_size + twice_size * twice_size)
    half = 0.5 + (0.5 * gap_size) * inverse
    half_inverse = lax.rsqrt(half)
    large = half * half_inverse
    small = (0.5 * twice_size) * inverse * half_inverse
    sign = jnp.where(twice < 0.0, -1.0, 1.0)
    ahead = gap >= 0.0
    return jnp.where(ahead, large, small), sign * jnp.where(ahead, small, large)


def row_copies(rows, index):
    return jnp.broadcast_to(rows[index : index + 1, :], (8, BLK))


def ahead_by_one(rows):
    return pltpu.roll(rows, 1, 1)


def jacobi_bands(uu, ul, lu, ll):
    last = BAND - 1
    is_first = lax.broadcasted_iota(jnp.int32, (BAND, BLK), 0) == 0
    row_ids = lax.broadcasted_iota(jnp.int32, (BAND, BLK), 0)
    one = jnp.where(row_ids == last, 1.0, 0.0).astype(F32)
    zero = jnp.zeros((BAND, BLK), F32)
    u_top, u_low, l_top, l_low = one, zero, zero, one
    u_diag, l_diag, coupling = row_copies(uu, 0), row_copies(ll, 0), row_copies(ul, 0)
    for step in range(STEPS):
        cos, sin = half_angle(u_diag - l_diag, 2.0 * coupling)
        final_step = step == STEPS - 1
        if not final_step:
            u_past, l_past, x_past = (ahead_by_one(v) for v in (u_diag, l_diag, coupling))
            cos_past, sin_past = ahead_by_one(cos), ahead_by_one(sin)
            u_diag, coupling = (
                cos * (cos * u_diag + sin * coupling) + sin * (cos * coupling + sin * l_diag),
                cos_past * (cos * row_copies(ul, 1) + sin * row_copies(ll, 1))
                - sin_past * (cos * row_copies(uu, 1) + sin * row_copies(lu, 1)),
            )
            l_diag = cos_past * (cos_past * l_past - sin_past * x_past) - sin_past * (
                cos_past * x_past - sin_past * u_past
            )
        cos_b = jnp.concatenate([cos] * (BAND // 8), axis=0)
        sin_b = jnp.concatenate([sin] * (BAND // 8), axis=0)
        u_top, l_top = u_top * cos_b + l_top * sin_b, l_top * cos_b - u_top * sin_b
        u_low, l_low = u_low * cos_b + l_low * sin_b, l_low * cos_b - u_low * sin_b
        if final_step:
            break
        cos_d = jnp.concatenate(
            [pltpu.roll(cos, 8 * i, 1, stride=1, stride_axis=0) for i in range(BAND // 8)], axis=0
        )
        sin_d = jnp.concatenate(
            [pltpu.roll(sin, 8 * i, 1, stride=1, stride_axis=0) for i in range(BAND // 8)], axis=0
        )
        uu, lu = uu * cos_b + lu * sin_b, lu * cos_b - uu * sin_b
        ul, ll = ul * cos_b + ll * sin_b, ll * cos_b - ul * sin_b
        uu, ul = uu * cos_d + ul * sin_d, ul * cos_d - uu * sin_d
        lu, ll = lu * cos_d + ll * sin_d, ll * cos_d - lu * sin_d
        ul = pltpu.roll(ul, last, 0)
        lu = jnp.where(is_first, ul, ahead_by_one(pltpu.roll(lu, 1, 0)))
        ll = ahead_by_one(ll)
        l_top = ahead_by_one(pltpu.roll(l_top, last, 0))
        l_low = ahead_by_one(pltpu.roll(l_low, last, 0))
    back = BLK - last
    l_top, l_low = pltpu.roll(l_top, back, 1), pltpu.roll(l_low, back, 1)
    return u_top, u_low, l_top, l_low


def turned_half(top, low, first):
    return jnp.concatenate((put_band(top, first), put_band(low, first)), axis=1)


def times_turned(tile, turned):
    high, low = split(tile)
    turned_high, turned_low = split(turned)
    last = ((1,), (1,))
    return mm(high, turned_high, last) + (mm(high, turned_low, last) + mm(low, turned_high, last))


def all_bands(gram):
    rows = []
    for top in (0, BLK):
        for left in (0, BLK):
            rows += bands_of(gram[top : top + BLK, left : left + BLK], BAND)
    return jnp.concatenate(rows, axis=0)


def summed(parts_ref):
    total = parts_ref[0]
    for i in range(1, parts_ref.shape[0]):
        total = total + parts_ref[i]
    return total


def blocks(bands):
    return [bands[BAND * i : BAND * (i + 1)] for i in range(4)]


VMEM_SPEC = pl.BlockSpec(memory_space=pltpu.VMEM)
PARAMS = pltpu.CompilerParams(vmem_limit_bytes=LIMIT)


def gram_kernel(cols_ref, bands_ref, early_ref, sem):
    copy = pltpu.make_async_copy(cols_ref.at[pl.ds(0, EARLY)], early_ref, sem)
    copy.start()
    bands_ref[...] = all_bands(gram_tile(cols_ref[...]))
    copy.wait()


def gram_bands(cols):
    return pl.pallas_call(
        gram_kernel,
        in_specs=[VMEM_SPEC],
        out_specs=(VMEM_SPEC, pl.BlockSpec(memory_space=pltpu.HBM)),
        out_shape=(
            jax.ShapeDtypeStruct((ROWS, BLK), F32),
            jax.ShapeDtypeStruct((EARLY, 2 * BLK), F32),
        ),
        scratch_shapes=[pltpu.SemaphoreType.DMA(())],
        compiler_params=PARAMS,
        name="gram_bands",
    )(cols)


def jacobi_kernel(parts_ref, own_ref, trace_ref):
    bands = summed(parts_ref)
    uu, ul, lu, ll = blocks(bands)
    trace_ref[...] = jnp.broadcast_to((uu[:1] + ll[:1])[None], trace_ref.shape)
    own_ref[...] = jnp.concatenate(jacobi_bands(uu, ul, lu, ll), axis=0)


def jacobi(parts, copies):
    return pl.pallas_call(
        jacobi_kernel,
        in_specs=[VMEM_SPEC],
        out_shape=(
            pltpu.VMEM((ROWS, BLK), F32),
            jax.ShapeDtypeStruct((copies, 1, BLK), F32),
        ),
        name="jacobi",
    )(parts)


def own_kernel(cols_ref, own_ref, upper_ref, late_ref):
    u_top, u_low, l_top, l_low = blocks(own_ref[...])
    late_ref[: 2 * BAND, :] = own_ref[2 * BAND :, :]
    late_ref[2 * BAND :, :] = times_turned(cols_ref[EARLY:, :], turned_half(l_top, l_low, 0))
    upper_ref[...] = times_turned(cols_ref[...], turned_half(u_top, u_low, 1 - BAND))


def own_halves(cols, own):
    rows = cols.shape[0]
    return pl.pallas_call(
        own_kernel,
        in_specs=[VMEM_SPEC, VMEM_SPEC],
        out_shape=(
            jax.ShapeDtypeStruct((rows, BLK), F32),
            jax.ShapeDtypeStruct((2 * BAND + rows - EARLY, BLK), F32),
        ),
        cost_estimate=COST,
        compiler_params=PARAMS,
        name="own_halves",
    )(cols, own)


def link_kernel(raw_ref, late_ref, upper_ref, lower_ref, bands_ref, turned_ref, total_ref):
    step = pl.program_id(0)

    @pl.when(step == 0)
    def _():
        turned_ref[...] = turned_half(late_ref[:BAND, :], late_ref[BAND : 2 * BAND, :], 0)
        total_ref[...] = jnp.zeros_like(total_ref)

    tile = raw_ref.shape[0]
    rows = pl.ds(pl.multiple_of(step * tile, 8), tile)
    lower = times_turned(raw_ref[...], turned_ref[...])
    lower_ref[rows, :] = lower
    total_ref[...] += gram_tile(jnp.concatenate((upper_ref[rows, :], lower), axis=1))

    @pl.when(step == pl.num_programs(0) - 1)
    def _():
        late = late_ref[2 * BAND :, :]
        lower_ref[EARLY:, :] = late
        gram = gram_tile(jnp.concatenate((upper_ref[EARLY:, :], late), axis=1))
        bands_ref[...] = all_bands(total_ref[...] + gram)


def link(raw, late, upper):
    rows = upper.shape[0]
    return pl.pallas_call(
        link_kernel,
        grid=(2,),
        in_specs=[
            pl.BlockSpec((EARLY // 2, 2 * BLK), lambda i: (i, 0)),
            pl.BlockSpec(late.shape, lambda i: (0, 0)),
            pl.BlockSpec(upper.shape, lambda i: (0, 0)),
        ],
        out_specs=(
            pl.BlockSpec((rows, BLK), lambda i: (0, 0)),
            pl.BlockSpec((ROWS, BLK), lambda i: (0, 0)),
        ),
        out_shape=(
            jax.ShapeDtypeStruct((rows, BLK), F32),
            jax.ShapeDtypeStruct((ROWS, BLK), F32),
        ),
        scratch_shapes=[pltpu.VMEM((BLK, 2 * BLK), F32), pltpu.VMEM((2 * BLK, 2 * BLK), F32)],
        cost_estimate=COST,
        compiler_params=PARAMS,
        name="link",
    )(raw, late, upper)


def final_kernel(entry_count, parts_ref, traces_ref, upper_ref, lower_ref, out_ref, turned_ref):
    @pl.when(pl.program_id(0) == 0)
    def _():
        rms = jnp.sqrt(jnp.sum(summed(traces_ref), axis=1, keepdims=True) / entry_count)
        u_top, u_low, l_top, l_low = jacobi_bands(*blocks(summed(parts_ref)))
        turned_ref[:BLK, :] = turned_half(u_top, u_low, 1 - BAND) / rms
        turned_ref[BLK:, :] = turned_half(l_top, l_low, 0) / rms

    pair = jnp.concatenate((upper_ref[...], lower_ref[...]), axis=1)
    out_ref[...] = times_turned(pair, turned_ref[...])


def final(entry_count, parts, traces, upper, lower):
    rows = upper.shape[0]
    half_spec = pl.BlockSpec((TILE, BLK), lambda i: (i, 0))
    return pl.pallas_call(
        functools.partial(final_kernel, entry_count),
        grid=(rows // TILE,),
        in_specs=[
            pl.BlockSpec(parts.shape, lambda i: (0, 0, 0)),
            pl.BlockSpec(traces.shape, lambda i: (0, 0, 0)),
            half_spec,
            half_spec,
        ],
        out_specs=pl.BlockSpec((TILE, 2 * BLK), lambda i: (i, 0)),
        out_shape=jax.ShapeDtypeStruct((rows, 2 * BLK), F32),
        scratch_shapes=[pltpu.VMEM((2 * BLK, 2 * BLK), F32)],
        compiler_params=PARAMS,
        name="final",
    )(parts, traces, upper, lower)


def to_next(value):
    count = lax.axis_size("pair")
    return lax.ppermute(value, "pair", [(pair, (pair + 1) % count) for pair in range(count)])


def body(activations):
    pairs, rows = lax.axis_size("pair"), lax.axis_size("row")
    entry_count = activations.shape[0] * activations.shape[1] * pairs * rows

    bands, early = gram_bands(activations)
    raw = to_next(early)
    own, traces = jacobi(lax.all_gather(bands, "row"), pairs)
    upper, late = own_halves(activations, own)
    late = to_next(late)
    traces = lax.all_to_all(traces, "pair", 0, 0, tiled=True)
    lower, bands = link(raw, late, upper)
    bands, traces = lax.optimization_barrier((bands, traces))
    parts = lax.all_gather(bands, "row")
    return final(float(entry_count), parts, traces, upper, lower)


def solution(mesh):
    return jax.shard_map(
        body,
        mesh=mesh,
        in_specs=(P("row", "pair"),),
        out_specs=P("row", "pair"),
        check_vma=False,
    )
```

time: 114 us -> 83 us (0.73)
  blocking collectives: 75.1 us -> 45 us
  Pallas kernels: 28.3 us -> 15 us
  starting transfers between devices: 3.22 us -> 15.1 us
  waiting for transfers between devices: 0.01 us -> 5.94 us
  other arithmetic: 4.69 us -> 0 us
    all_to_all x1 -> x0, blocking collectives: 29.1 us -> none  [to_all(): return lax.all_to_all(copies, axis, 0, 0, tiled=True)]
    pallas_call x6 -> x5, Pallas kernels: 28.3 us -> 15 us  [the longest x1 4.73 us: link(): pl.pallas_call(link_kernel, grid=(2,), in_specs=[pl.BlockSpec((EARLY // 2...]
    all_to_all x0 -> x1, starting transfers between devices: none -> 7.88 us  [body(): traces = lax.all_to_all(traces, 'pair', 0, 0, tiled=True)]
    ppermute x1 -> x2, waiting for transfers between devices: 0.01 us -> 5.94 us  [to_next(): lax.ppermute(value, 'pair', [(pair, (pair + 1) % count) for pair in range...]
    ppermute x1 -> x2, starting transfers between devices: 3.22 us -> 7.22 us  [to_next(): lax.ppermute(value, 'pair', [(pair, (pair + 1) % count) for pair in range...]
    div x1 -> x0, other arithmetic: 1.7 us -> none  [body(): return rotate(pair_two, jacobi(parts_two) / rms_value)]
    slice x1 -> x0, local copies, waits for them, and re-layouts: 1.68 us -> none  [body(): pair_two = jnp.concatenate((rotated_one[:, :BLK], arrived), axis=1)]
    unnamed x0 -> x4, local copies, waits for them, and re-layouts: none -> 1.59 us
  transfers between devices with their start and end apart: 1 -> 3, of which waited for: 0 -> 1; matrix products, arithmetic and copies ran while one was open for 1% -> 0% of each run, Pallas kernels for 0% -> 11%
where the time goes in v3:
time: 83 us; the launch traced here: 82.6 us
  blocking collectives  45 us (54%)
  starting transfers between devices  15.1 us (18%)
  Pallas kernels  15 us (18%)
  waiting for transfers between devices  5.94 us (7%)
  local copies, waits for them, and re-layouts  1.59 us (2%)
    all_gather x1, blocking collectives, body(): own, traces = jacobi(lax.all_gather(bands, 'row'), pairs)  26.8 us
    all_gather x1, blocking collectives, body(): parts = lax.all_gather(bands, 'row')  18.2 us
    all_to_all x1, starting transfers between devices, body(): traces = lax.all_to_all(traces, 'pair', 0, 0, tiled=True)  7.88 us
    ppermute x2, starting transfers between devices, to_next(): lax.ppermute(value, 'pair', [(pair, (pair + 1) % count) for pair in range...  7.22 us
    ppermute x2, waiting for transfers between devices, to_next(): lax.ppermute(value, 'pair', [(pair, (pair + 1) % count) for pair in range...  5.94 us
    pallas_call x1, Pallas kernels, link(): pl.pallas_call(link_kernel, grid=(2,), in_specs=[pl.BlockSpec((EARLY // 2...  4.73 us
    pallas_call x1, Pallas kernels, final(): pl.pallas_call(functools.partial(final_kernel, entry_count), grid=(rows /...  4.21 us
    pallas_call x1, Pallas kernels, jacobi(): pl.pallas_call(jacobi_kernel, in_specs=[VMEM_SPEC], out_shape=(pltpu.VMEM...  2.75 us
  transfers between devices with their start and end apart: 3, of which 1 were waited for; matrix products, arithmetic and copies ran while one was open for 0% of the time, Pallas kernels for 11%

profile of v3, /device:TPU:1, one launch (start us, length us, event | category | flops | bytes accessed | tf_op | source)
XLA Modules:
  0.0 82.6 jit_solution(15182313660969737389)
XLA Ops:
  0.0 0.0 copy-start
  0.0 1.6 %copy-done = f32[2048,256]{1,0:T(8,128)S(1)} copy-done((f32[2048,256]{1,0:T(8,128)S(1)}, f32[2048,256]{1,0:T(8,128)}, u32[]{:S(2)}) %copy-start) | copy-done | bytes 2097176
  1.6 0.0 copy-start.1
  1.6 1.4 %gram_bands.1 = (f32[64,128]{1,0:T(8,128)S(1)}, f32[1216,256]{1,0:T(8,128)}) custom-call(f32[2048,256]{1,0:T(8,128)S(1)} %copy-done), custom_call_target="tpu_custom_call" | custom-call | tf_op jit(solution)/shard_map/gram_bands/pallas_call | solution.py:177
  3.0 4.0 %collective-permute-start = (f32[1216,256]{1,0:T(8,128)}, f32[1216,256]{1,0:T(8,128)}, u32[]{:S(2)}, u32[]{:S(2)}) collective-permute-start(f32[1216,256]{1,0:T(8,128)} %get-tuple-element.15), channel_id=1, source_target_pairs={{0,16},{16,32},{32,48},{48,64},{64,80},{80,96},{96,112},{112,128},... | collective-permute-start | bytes 3735560 | tf_op jit(solution)/shard_map/ppermute | solution.py:313
  7.1 26.8 %all-gather = f32[1024,128]{1,0:T(8,128)} all-gather(f32[64,128]{1,0:T(8,128)S(1)} %get-tuple-element.16), channel_id=2, replica_groups=mesh['pair'=32,'row'=16] {'row'}, dimensions={0}, use_global_device_ids=true | all-gather | bytes 557056 | tf_op jit(solution)/shard_map/all_gather | solution.py:322
  33.9 2.8 %jacobi.1 = (f32[64,128]{1,0:T(8,128)S(1)}, f32[32,1,128]{2,1,0:T(1,128)}) custom-call(f32[16,64,128]{2,1,0:T(8,128)} %bitcast.3), custom_call_target="tpu_custom_call" | custom-call | tf_op jit(solution)/shard_map/jacobi/pallas_call | solution.py:199
  36.6 0.0 copy-done.1
  36.6 1.8 %own_halves.1 = (f32[2048,128]{1,0:T(8,128)S(1)}, f32[864,128]{1,0:T(8,128)}) custom-call(f32[2048,256]{1,0:T(8,128)S(1)} %copy-done.1, f32[64,128]{1,0:T(8,128)S(1)} %get-tuple-element.17.own_ref), custom_call_target="tpu_custom_call" | custom-call | flops 2000000000 | bytes 6000000 | tf_op jit(solution)/shard_map/own_halves/pallas_call | solution.py:219
  38.5 3.2 %collective-permute-start.1 = (f32[864,128]{1,0:T(8,128)}, f32[864,128]{1,0:T(8,128)S(1)}, u32[]{:S(2)}, u32[]{:S(2)}) collective-permute-start(f32[864,128]{1,0:T(8,128)} %get-tuple-element.18), channel_id=1, source_target_pairs={{0,16},{16,32},{32,48},{48,64},{64,80},{80,96},{96,112},{112,128},... | collective-permute-start | bytes 1327112 | tf_op jit(solution)/shard_map/ppermute | solution.py:313
  41.7 7.9 %all-to-all-start = ((f32[32,1,128]{2,1,0:T(1,128)}), f32[32,1,128]{2,1,0:T(1,128)S(1)}, u32[]{:S(2)}, u32[]{:S(2)}) async-start(f32[32,1,128]{2,1,0:T(1,128)} %get-tuple-element.21), calls=%async_computation | async-start | bytes 32768 | tf_op jit(solution)/shard_map/all_to_all | solution.py:325
  49.5 5.9 %collective-permute-done.1.late_ref = f32[864,128]{1,0:T(8,128)S(1)} collective-permute-done((f32[864,128]{1,0:T(8,128)}, f32[864,128]{1,0:T(8,128)S(1)}, u32[]{:S(2)}, u32[]{:S(2)}) %collective-permute-start.1) | collective-permute-done | bytes 442400 | tf_op jit(solution)/shard_map/ppermute | solution.py:313
  55.5 0.0 collective-permute-done.raw_ref
  55.5 4.7 %link.1 = (f32[2048,128]{1,0:T(8,128)S(1)}, f32[64,128]{1,0:T(8,128)S(1)}) custom-call(f32[1216,256]{1,0:T(8,128)} %collective-permute-done.raw_ref, f32[864,128]{1,0:T(8,128)S(1)} %collective-permute-done.1.late_ref, f32[2048,128]{1,0:T(8,128)S(1)} %get-tuple-element.19.upper_ref), custom_call_target="tpu_custom_call" | custom-call | flops 2000000000 | bytes 6000000 | tf_op jit(solution)/shard_map/link/pallas_call | solution.py:256
  60.2 0.0 all-to-all-done.traces_ref
  60.2 18.2 %all-gather.1 = f32[1024,128]{1,0:T(8,128)S(1)} all-gather(f32[64,128]{1,0:T(8,128)S(1)} %get-tuple-element.22), channel_id=3, replica_groups=mesh['pair'=32,'row'=16] {'row'}, dimensions={0}, use_global_device_ids=true | all-gather | bytes 557056 | tf_op jit(solution)/shard_map/all_gather | solution.py:328
  78.4 4.2 %final.1 = f32[2048,256]{1,0:T(8,128)} custom-call(f32[16,64,128]{2,1,0:T(8,128)S(1)} %bitcast.2, f32[32,1,128]{2,1,0:T(1,128)S(1)} %all-to-all-done.traces_ref, f32[2048,128]{1,0:T(8,128)S(1)} %get-tuple-element.19.upper_ref, f32[2048,128]{1,0:T(8,128)S(1)} %get-tuple-element.24.lower_ref), custom_call_target="tpu_custom_call" | custom-call | tf_op jit(solution)/shard_map/final/pallas_call | solution.py:294
Async XLA Ops:
  0.0 1.6 %copy-start = (f32[2048,256]{1,0:T(8,128)S(1)}, f32[2048,256]{1,0:T(8,128)}, u32[]{:S(2)}) copy-start(f32[2048,256]{1,0:T(8,128)} %cols_ref.3) | copy-start | bytes 6291460
  1.6 35.0 %copy-start.1 = (f32[2048,256]{1,0:T(8,128)S(1)}, f32[2048,256]{1,0:T(8,128)}, u32[]{:S(2)}) copy-start(f32[2048,256]{1,0:T(8,128)} %cols_ref.3) | copy-start | bytes 6291460
  3.0 52.5 %collective-permute-start = (f32[1216,256]{1,0:T(8,128)}, f32[1216,256]{1,0:T(8,128)}, u32[]{:S(2)}, u32[]{:S(2)}) collective-permute-start(f32[1216,256]{1,0:T(8,128)} %get-tuple-element.15), channel_id=1, source_target_pairs={{0,16},{16,32},{32,48},{48,64},{64,80},{80,96},{96,112},{112,128},... | collective-permute-start | bytes 3735560 | tf_op jit(solution)/shard_map/ppermute | solution.py:313
  38.5 17.0 %collective-permute-start.1 = (f32[864,128]{1,0:T(8,128)}, f32[864,128]{1,0:T(8,128)S(1)}, u32[]{:S(2)}, u32[]{:S(2)}) collective-permute-start(f32[864,128]{1,0:T(8,128)} %get-tuple-element.18), channel_id=1, source_target_pairs={{0,16},{16,32},{32,48},{48,64},{64,80},{80,96},{96,112},{112,128},... | collective-permute-start | bytes 1327112 | tf_op jit(solution)/shard_map/ppermute | solution.py:313
  41.7 18.6 %all-to-all-start = ((f32[32,1,128]{2,1,0:T(1,128)}), f32[32,1,128]{2,1,0:T(1,128)S(1)}, u32[]{:S(2)}, u32[]{:S(2)}) async-start(f32[32,1,128]{2,1,0:T(1,128)} %get-tuple-element.21), calls=%async_computation | async-start | bytes 32768 | tf_op jit(solution)/shard_map/all_to_all | solution.py:325

commit v4 on v3

--- a/solution.py
+++ b/solution.py
@@ -12,7 +12,8 @@
 BAND = 16
 ROWS = 4 * BAND
 TILE = 1024
-EARLY = 1216
+EARLY = 1152
+PART = 512
 LIMIT = 24 << 20
 COST = pl.CostEstimate(flops=2_000_000_000, bytes_accessed=6_000_000, transcendentals=0)
 F32 = jnp.float32
@@ -166,92 +167,135 @@
 PARAMS = pltpu.CompilerParams(vmem_limit_bytes=LIMIT)
 
 
-def gram_kernel(cols_ref, bands_ref, early_ref, sem):
-    copy = pltpu.make_async_copy(cols_ref.at[pl.ds(0, EARLY)], early_ref, sem)
-    copy.start()
+def early_kernel(cols_ref, early_ref, sems):
+    step = EARLY // sems.shape[0]
+    copies = [
+        pltpu.make_async_copy(
+            cols_ref.at[pl.ds(i * step, step)], early_ref.at[pl.ds(i * step, step)], sems.at[i]
+        )
+        for i in range(sems.shape[0])
+    ]
+    for copy in copies:
+        copy.start()
+    for copy in copies:
+        copy.wait()
+
+
+def early_rows(cols):
+    return pl.pallas_call(
+        early_kernel,
+        in_specs=[pl.BlockSpec(memory_space=pltpu.HBM)],
+        out_specs=VMEM_SPEC,
+        out_shape=pltpu.VMEM((EARLY, 2 * BLK), F32),
+        scratch_shapes=[pltpu.SemaphoreType.DMA((4,))],
+        name="early_rows",
+    )(cols)
+
+
+def gram_kernel(cols_ref, bands_ref):
     bands_ref[...] = all_bands(gram_tile(cols_ref[...]))
-    copy.wait()
 
 
 def gram_bands(cols):
     return pl.pallas_call(
         gram_kernel,
         in_specs=[VMEM_SPEC],
-        out_specs=(VMEM_SPEC, pl.BlockSpec(memory_space=pltpu.HBM)),
-        out_shape=(
-            jax.ShapeDtypeStruct((ROWS, BLK), F32),
-            jax.ShapeDtypeStruct((EARLY, 2 * BLK), F32),
-        ),
-        scratch_shapes=[pltpu.SemaphoreType.DMA(())],
+        out_shape=jax.ShapeDtypeStruct((ROWS, BLK), F32),
         compiler_params=PARAMS,
         name="gram_bands",
     )(cols)
 
 
-def jacobi_kernel(parts_ref, own_ref, trace_ref):
+def jacobi_kernel(parts_ref, cols_ref, own_ref, late_ref, trace_ref):
     bands = summed(parts_ref)
     uu, ul, lu, ll = blocks(bands)
     trace_ref[...] = jnp.broadcast_to((uu[:1] + ll[:1])[None], trace_ref.shape)
-    own_ref[...] = jnp.concatenate(jacobi_bands(uu, ul, lu, ll), axis=0)
-
-
-def jacobi(parts, copies):
+    u_top, u_low, l_top, l_low = jacobi_bands(uu, ul, lu, ll)
+    own_ref[...] = jnp.concatenate((u_top, u_low), axis=0)
+    late_ref[: 2 * BAND, :] = jnp.concatenate((l_top, l_low), axis=0)
+    late_ref[2 * BAND :, :] = times_turned(cols_ref[EARLY:, :], turned_half(l_top, l_low, 0))
+
+
+def jacobi(parts, cols, copies):
     return pl.pallas_call(
         jacobi_kernel,
-        in_specs=[VMEM_SPEC],
+        in_specs=[VMEM_SPEC, VMEM_SPEC],
         out_shape=(
-            pltpu.VMEM((ROWS, BLK), F32),
+            pltpu.VMEM((2 * BAND, BLK), F32),
+            jax.ShapeDtypeStruct((2 * BAND + cols.shape[0] - EARLY, BLK), F32),
             jax.ShapeDtypeStruct((copies, 1, BLK), F32),
         ),
+        compiler_params=PARAMS,
         name="jacobi",
-    )(parts)
-
-
-def own_kernel(cols_ref, own_ref, upper_ref, late_ref):
-    u_top, u_low, l_top, l_low = blocks(own_ref[...])
-    late_ref[: 2 * BAND, :] = own_ref[2 * BAND :, :]
-    late_ref[2 * BAND :, :] = times_turned(cols_ref[EARLY:, :], turned_half(l_top, l_low, 0))
-    upper_ref[...] = times_turned(cols_ref[...], turned_half(u_top, u_low, 1 - BAND))
-
-
-def own_halves(cols, own):
-    rows = cols.shape[0]
-    return pl.pallas_call(
-        own_kernel,
+    )(parts, cols)
+
+
+def upper_kernel(cols_ref, own_ref, upper_ref, bands_ref):
+    upper = times_turned(cols_ref[...], turned_half(own_ref[:BAND, :], own_ref[BAND:, :], 1 - BAND))
+    upper_ref[...] = upper
+    high, low = split(upper)
+    rows = ((0,), (0,))
+    cross = mm(high, low, rows)
+    gram = mm(high, high, rows) + mm(low, low, rows) + (cross + cross.T)
+    bands_ref[...] = jnp.concatenate(bands_of(gram, BAND), axis=0)
+
+
+def upper_half(cols, own):
+    return pl.pallas_call(
+        upper_kernel,
         in_specs=[VMEM_SPEC, VMEM_SPEC],
         out_shape=(
-            jax.ShapeDtypeStruct((rows, BLK), F32),
-            jax.ShapeDtypeStruct((2 * BAND + rows - EARLY, BLK), F32),
+            jax.ShapeDtypeStruct((cols.shape[0], BLK), F32),
+            jax.ShapeDtypeStruct((BAND, BLK), F32),
         ),
         cost_estimate=COST,
         compiler_params=PARAMS,
-        name="own_halves",
+        name="upper_half",
     )(cols, own)
 
 
-def link_kernel(raw_ref, late_ref, upper_ref, lower_ref, bands_ref, turned_ref, total_ref):
+def lower_gram(upper, lower):
+    low_high, low_low = split(lower)
+    pair_high, pair_low = split(jnp.concatenate((upper, lower), axis=1))
+    rows = ((0,), (0,))
+    return (
+        mm(low_high, pair_high, rows)
+        + mm(low_low, pair_low, rows)
+        + (mm(low_high, pair_low, rows) + mm(low_low, pair_high, rows))
+    )
+
+
+def link_kernel(raw_ref, late_ref, upper_ref, uu_ref, pair_ref, bands_ref, turned_ref, total_ref):
     step = pl.program_id(0)
 
     @pl.when(step == 0)
     def _():
         turned_ref[...] = turned_half(late_ref[:BAND, :], late_ref[BAND : 2 * BAND, :], 0)
-        total_ref[...] = jnp.zeros_like(total_ref)
+        late = late_ref[2 * BAND :, :]
+        upper = upper_ref[EARLY:, :]
+        pair_ref[EARLY:, :BLK] = upper
+        pair_ref[EARLY:, BLK:] = late
+        total_ref[...] = lower_gram(upper, late)
 
     tile = raw_ref.shape[0]
     rows = pl.ds(pl.multiple_of(step * tile, 8), tile)
     lower = times_turned(raw_ref[...], turned_ref[...])
-    lower_ref[rows, :] = lower
-    total_ref[...] += gram_tile(jnp.concatenate((upper_ref[rows, :], lower), axis=1))
+    upper = upper_ref[rows, :]
+    pair_ref[rows, :BLK] = upper
+    pair_ref[rows, BLK:] = lower
+    total_ref[...] += lower_gram(upper, lower)
 
     @pl.when(step == pl.num_programs(0) - 1)
     def _():
-        late = late_ref[2 * BAND :, :]
-        lower_ref[EARLY:, :] = late
-        gram = gram_tile(jnp.concatenate((upper_ref[EARLY:, :], late), axis=1))
-        bands_ref[...] = all_bands(total_ref[...] + gram)
-
-
-def link(raw, late, upper):
+        total = total_ref[...]
+        lu, ll = total[:, :BLK], total[:, BLK:]
+        bands_ref[:BAND, :] = uu_ref[...]
+        bands_ref[BAND:, :] = jnp.concatenate(
+            bands_of(lu.T, BAND) + bands_of(lu, BAND) + bands_of(ll, BAND), axis=0
+        )
+
+
+def link(raw, late, upper, uu):
     rows = upper.shape[0]
     return pl.pallas_call(
         link_kernel,
@@ -260,52 +304,67 @@
             pl.BlockSpec((EARLY // 2, 2 * BLK), lambda i: (i, 0)),
             pl.BlockSpec(late.shape, lambda i: (0, 0)),
             pl.BlockSpec(upper.shape, lambda i: (0, 0)),
+            pl.BlockSpec(uu.shape, lambda i: (0, 0)),
         ],
         out_specs=(
-            pl.BlockSpec((rows, BLK), lambda i: (0, 0)),
+            pl.BlockSpec((rows, 2 * BLK), lambda i: (0, 0)),
             pl.BlockSpec((ROWS, BLK), lambda i: (0, 0)),
         ),
         out_shape=(
-            jax.ShapeDtypeStruct((rows, BLK), F32),
+            jax.ShapeDtypeStruct((rows, 2 * BLK), F32),
             jax.ShapeDtypeStruct((ROWS, BLK), F32),
         ),
-        scratch_shapes=[pltpu.VMEM((BLK, 2 * BLK), F32), pltpu.VMEM((2 * BLK, 2 * BLK), F32)],
+        scratch_shapes=[pltpu.VMEM((BLK, 2 * BLK), F32), pltpu.VMEM((BLK, 2 * BLK), F32)],
         cost_estimate=COST,
         compiler_params=PARAMS,
         name="link",
-    )(raw, late, upper)
-
-
-def final_kernel(entry_count, parts_ref, traces_ref, upper_ref, lower_ref, out_ref, turned_ref):
-    @pl.when(pl.program_id(0) == 0)
-    def _():
-        rms = jnp.sqrt(jnp.sum(summed(traces_ref), axis=1, keepdims=True) / entry_count)
-        u_top, u_low, l_top, l_low = jacobi_bands(*blocks(summed(parts_ref)))
-        turned_ref[:BLK, :] = turned_half(u_top, u_low, 1 - BAND) / rms
-        turned_ref[BLK:, :] = turned_half(l_top, l_low, 0) / rms
-
-    pair = jnp.concatenate((upper_ref[...], lower_ref[...]), axis=1)
-    out_ref[...] = times_turned(pair, turned_ref[...])
-
-
-def final(entry_count, parts, traces, upper, lower):
-    rows = upper.shape[0]
-    half_spec = pl.BlockSpec((TILE, BLK), lambda i: (i, 0))
+    )(raw, late, upper, uu)
+
+
+def final_kernel(
+    entry_count, parts_ref, traces_ref, pair_ref, out_ref, tiles_ref, high_ref, low_ref, sems
+):
+    rms = jnp.sqrt(jnp.sum(summed(traces_ref), axis=1, keepdims=True) / entry_count)
+    u_top, u_low, l_top, l_low = jacobi_bands(*blocks(summed(parts_ref)))
+    for first, turned in (
+        (0, turned_half(u_top, u_low, 1 - BAND)),
+        (BLK, turned_half(l_top, l_low, 0)),
+    ):
+        high, low = split(turned / rms)
+        high_ref[first : first + BLK, :] = high
+        low_ref[first : first + BLK, :] = low
+    last = ((1,), (1,))
+    stores = []
+    for i in range(tiles_ref.shape[0]):
+        rows = pl.ds(i * PART, PART)
+        high, low = split(pair_ref[rows, :])
+        tiles_ref[i] = mm(high, high_ref[...], last) + (
+            mm(high, low_ref[...], last) + mm(low, high_ref[...], last)
+        )
+        store = pltpu.make_async_copy(tiles_ref.at[i], out_ref.at[rows], sems.at[i])
+        store.start()
+        stores.append(store)
+    for store in stores:
+        store.wait()
+
+
+def final(entry_count, parts, traces, pair):
+    rows = pair.shape[0]
+    count = rows // PART
     return pl.pallas_call(
         functools.partial(final_kernel, entry_count),
-        grid=(rows // TILE,),
-        in_specs=[
-            pl.BlockSpec(parts.shape, lambda i: (0, 0, 0)),
-            pl.BlockSpec(traces.shape, lambda i: (0, 0, 0)),
-            half_spec,
-            half_spec,
+        in_specs=[VMEM_SPEC] * 3,
+        out_specs=pl.BlockSpec(memory_space=pltpu.HBM),
+        out_shape=jax.ShapeDtypeStruct((rows, 2 * BLK), F32),
+        scratch_shapes=[
+            pltpu.VMEM((count, PART, 2 * BLK), F32),
+            pltpu.VMEM((2 * BLK, 2 * BLK), BF16),
+            pltpu.VMEM((2 * BLK, 2 * BLK), BF16),
+            pltpu.SemaphoreType.DMA((count,)),
         ],
-        out_specs=pl.BlockSpec((TILE, 2 * BLK), lambda i: (i, 0)),
-        out_shape=jax.ShapeDtypeStruct((rows, 2 * BLK), F32),
-        scratch_shapes=[pltpu.VMEM((2 * BLK, 2 * BLK), F32)],
         compiler_params=PARAMS,
         name="final",
-    )(parts, traces, upper, lower)
+    )(parts, traces, pair)
 
 
 def to_next(value):
@@ -317,16 +376,16 @@
     pairs, rows = lax.axis_size("pair"), lax.axis_size("row")
     entry_count = activations.shape[0] * activations.shape[1] * pairs * rows
 
-    bands, early = gram_bands(activations)
-    raw = to_next(early)
-    own, traces = jacobi(lax.all_gather(bands, "row"), pairs)
-    upper, late = own_halves(activations, own)
+    raw = to_next(early_rows(activations))
+    bands = gram_bands(activations)
+    own, late, traces = jacobi(lax.all_gather(bands, "row"), activations, pairs)
     late = to_next(late)
     traces = lax.all_to_all(traces, "pair", 0, 0, tiled=True)
-    lower, bands = link(raw, late, upper)
+    upper, uu = upper_half(activations, own)
+    pair, bands = link(raw, late, upper, uu)
     bands, traces = lax.optimization_barrier((bands, traces))
     parts = lax.all_gather(bands, "row")
-    return final(float(entry_count), parts, traces, upper, lower)
+    return final(float(entry_count), parts, traces, pair)
 
 
 def solution(mesh):

time: 83 us -> 80.1 us (0.965)
  Pallas kernels: 15 us -> 17.1 us
  waiting for transfers between devices: 5.94 us -> 4.16 us
  blocking collectives: 45 us -> 43.4 us
  local copies, waits for them, and re-layouts: 1.59 us -> 0.01 us
    pallas_call x4 -> x5, Pallas kernels: 10.2 us -> 12.6 us  [the longest x1 3.99 us: final(): pl.pallas_call(functools.partial(final_kernel, entry_count), in_specs=[VM...]
    ppermute x2, waiting for transfers between devices: 5.94 us -> 4.16 us  [to_next(): lax.ppermute(value, 'pair', [(pair, (pair + 1) % count) for pair in range...]
    unnamed x4 -> x2, local copies, waits for them, and re-layouts: 1.59 us -> 0.01 us
    all_gather x1, blocking collectives: 26.8 us -> 25.4 us  [body(): own, late, traces = jacobi(lax.all_gather(bands, 'row'), activations, pairs)]
  transfers between devices with their start and end apart: 3 -> 3, of which waited for: 1 -> 1; matrix products, arithmetic and copies ran while one was open for 0% -> 0% of each run, Pallas kernels for 11% -> 15%
where the time goes in v4:
time: 80.1 us; the launch traced here: 79.9 us
  blocking collectives  43.4 us (54%)
  Pallas kernels  17.1 us (21%)
  starting transfers between devices  15.1 us (19%)
  waiting for transfers between devices  4.16 us (5%)
    all_gather x1, blocking collectives, body(): own, late, traces = jacobi(lax.all_gather(bands, 'row'), activations, pairs)  25.4 us
    all_gather x1, blocking collectives, body(): parts = lax.all_gather(bands, 'row')  18 us
    all_to_all x1, starting transfers between devices, body(): traces = lax.all_to_all(traces, 'pair', 0, 0, tiled=True)  7.88 us
    ppermute x2, starting transfers between devices, to_next(): lax.ppermute(value, 'pair', [(pair, (pair + 1) % count) for pair in range...  7.23 us
    pallas_call x1, Pallas kernels, link(): pl.pallas_call(link_kernel, grid=(2,), in_specs=[pl.BlockSpec((EARLY // 2...  4.56 us
    ppermute x2, waiting for transfers between devices, to_next(): lax.ppermute(value, 'pair', [(pair, (pair + 1) % count) for pair in range...  4.16 us
    pallas_call x1, Pallas kernels, final(): pl.pallas_call(functools.partial(final_kernel, entry_count), in_specs=[VM...  3.99 us
    pallas_call x1, Pallas kernels, jacobi(): pl.pallas_call(jacobi_kernel, in_specs=[VMEM_SPEC, VMEM_SPEC], out_shape=...  3.16 us
  transfers between devices with their start and end apart: 3, of which 1 were waited for; matrix products, arithmetic and copies ran while one was open for 0% of the time, Pallas kernels for 15%

profile of v4, /device:TPU:1, one launch (start us, length us, event | category | flops | bytes accessed | tf_op | source)
XLA Modules:
  0.0 79.9 jit_solution(14605917326179505707)
XLA Ops:
  0.0 0.0 copy-start
  0.0 1.4 %early_rows.1 = f32[1152,256]{1,0:T(8,128)S(1)} custom-call(f32[2048,256]{1,0:T(8,128)} %cols_ref.7), custom_call_target="tpu_custom_call" | custom-call | tf_op jit(solution)/shard_map/early_rows/pallas_call | solution.py:185
  1.4 4.0 %collective-permute-start = (f32[1152,256]{1,0:T(8,128)S(1)}, f32[1152,256]{1,0:T(8,128)}, u32[]{:S(2)}, u32[]{:S(2)}) collective-permute-start(f32[1152,256]{1,0:T(8,128)S(1)} %early_rows.1), channel_id=1, source_target_pairs={{0,16},{16,32},{32,48},{48,64},{64,80},{80,96},{96,112},{112,128},... | collective-permute-start | bytes 3538952 | tf_op jit(solution)/shard_map/ppermute | solution.py:372
  5.5 0.0 copy-done
  5.5 1.4 %gram_bands.1 = f32[64,128]{1,0:T(8,128)S(1)} custom-call(f32[2048,256]{1,0:T(8,128)S(1)} %copy-done), custom_call_target="tpu_custom_call" | custom-call | tf_op jit(solution)/shard_map/gram_bands/pallas_call | solution.py:200
  6.9 25.4 %all-gather = f32[1024,128]{1,0:T(8,128)S(1)} all-gather(f32[64,128]{1,0:T(8,128)S(1)} %gram_bands.1), channel_id=2, replica_groups=mesh['pair'=32,'row'=16] {'row'}, dimensions={0}, use_global_device_ids=true | all-gather | bytes 557056 | tf_op jit(solution)/shard_map/all_gather | solution.py:381
  32.3 3.2 %jacobi.1 = (f32[32,128]{1,0:T(8,128)S(1)}, f32[928,128]{1,0:T(8,128)}, f32[32,1,128]{2,1,0:T(1,128)}) custom-call(f32[16,64,128]{2,1,0:T(8,128)S(1)} %bitcast.2, f32[2048,256]{1,0:T(8,128)S(1)} %copy-done), custom_call_target="tpu_custom_call" | custom-call | tf_op jit(solution)/shard_map/jacobi/pallas_call | solution.py:220
  35.4 3.2 %collective-permute-start.1 = (f32[928,128]{1,0:T(8,128)}, f32[928,128]{1,0:T(8,128)}, u32[]{:S(2)}, u32[]{:S(2)}) collective-permute-start(f32[928,128]{1,0:T(8,128)} %get-tuple-element.14), channel_id=1, source_target_pairs={{0,16},{16,32},{32,48},{48,64},{64,80},{80,96},{96,112},{112,128},... | collective-permute-start | bytes 1425416 | tf_op jit(solution)/shard_map/ppermute | solution.py:372
  38.6 7.9 %all-to-all-start = ((f32[32,1,128]{2,1,0:T(1,128)}), f32[32,1,128]{2,1,0:T(1,128)S(1)}, u32[]{:S(2)}, u32[]{:S(2)}) async-start(f32[32,1,128]{2,1,0:T(1,128)} %get-tuple-element.19), calls=%async_computation | async-start | bytes 32768 | tf_op jit(solution)/shard_map/all_to_all | solution.py:383
  46.5 2.6 %upper_half.1 = (f32[2048,128]{1,0:T(8,128)S(1)}, f32[16,128]{1,0:T(8,128)S(1)}) custom-call(f32[2048,256]{1,0:T(8,128)S(1)} %copy-done, f32[32,128]{1,0:T(8,128)S(1)} %get-tuple-element.15.own_ref), custom_call_target="tpu_custom_call" | custom-call | flops 2000000000 | bytes 6000000 | tf_op jit(solution)/shard_map/upper_half/pallas_call | solution.py:244
  49.1 4.2 %collective-permute-done.1.late_ref = f32[928,128]{1,0:T(8,128)} collective-permute-done((f32[928,128]{1,0:T(8,128)}, f32[928,128]{1,0:T(8,128)}, u32[]{:S(2)}, u32[]{:S(2)}) %collective-permute-start.1) | collective-permute-done | bytes 475168 | tf_op jit(solution)/shard_map/ppermute | solution.py:372
  53.3 0.0 collective-permute-done.raw_ref
  53.3 4.6 %link.1 = (f32[2048,256]{1,0:T(8,128)S(1)}, f32[64,128]{1,0:T(8,128)S(1)}) custom-call(f32[1152,256]{1,0:T(8,128)} %collective-permute-done.raw_ref, f32[928,128]{1,0:T(8,128)} %collective-permute-done.1.late_ref, f32[2048,128]{1,0:T(8,128)S(1)} %get-tuple-element.16.upper_ref, f32[16,128]{1,0:T(8,128)S(1)} %get-tuple-element.17.uu_ref), custom_call_target="tpu_custom_call" | custom-call | flops 2000000000 | bytes 6000000 | tf_op jit(solution)/shard_map/link/pallas_call | solution.py:300
  57.9 0.0 all-to-all-done.traces_ref
  57.9 18.0 %all-gather.1 = f32[1024,128]{1,0:T(8,128)S(1)} all-gather(f32[64,128]{1,0:T(8,128)S(1)} %get-tuple-element.20), channel_id=3, replica_groups=mesh['pair'=32,'row'=16] {'row'}, dimensions={0}, use_global_device_ids=true | all-gather | bytes 557056 | tf_op jit(solution)/shard_map/all_gather | solution.py:387
  75.9 4.0 %final.1 = f32[2048,256]{1,0:T(8,128)} custom-call(f32[16,64,128]{2,1,0:T(8,128)S(1)} %bitcast.3, f32[32,1,128]{2,1,0:T(1,128)S(1)} %all-to-all-done.traces_ref, f32[2048,256]{1,0:T(8,128)S(1)} %get-tuple-element.22.pair_ref), custom_call_target="tpu_custom_call" | custom-call | tf_op jit(solution)/shard_map/final/pallas_call | solution.py:354
Async XLA Ops:
  0.0 5.5 %copy-start = (f32[2048,256]{1,0:T(8,128)S(1)}, f32[2048,256]{1,0:T(8,128)}, u32[]{:S(2)}) copy-start(f32[2048,256]{1,0:T(8,128)} %cols_ref.7) | copy-start | bytes 6291460
  1.4 51.9 %collective-permute-start = (f32[1152,256]{1,0:T(8,128)S(1)}, f32[1152,256]{1,0:T(8,128)}, u32[]{:S(2)}, u32[]{:S(2)}) collective-permute-start(f32[1152,256]{1,0:T(8,128)S(1)} %early_rows.1), channel_id=1, source_target_pairs={{0,16},{16,32},{32,48},{48,64},{64,80},{80,96},{96,112},{112,128},... | collective-permute-start | bytes 3538952 | tf_op jit(solution)/shard_map/ppermute | solution.py:372
  35.4 17.8 %collective-permute-start.1 = (f32[928,128]{1,0:T(8,128)}, f32[928,128]{1,0:T(8,128)}, u32[]{:S(2)}, u32[]{:S(2)}) collective-permute-start(f32[928,128]{1,0:T(8,128)} %get-tuple-element.14), channel_id=1, source_target_pairs={{0,16},{16,32},{32,48},{48,64},{64,80},{80,96},{96,112},{112,128},... | collective-permute-start | bytes 1425416 | tf_op jit(solution)/shard_map/ppermute | solution.py:372
  38.6 19.2 %all-to-all-start = ((f32[32,1,128]{2,1,0:T(1,128)}), f32[32,1,128]{2,1,0:T(1,128)S(1)}, u32[]{:S(2)}, u32[]{:S(2)}) async-start(f32[32,1,128]{2,1,0:T(1,128)} %get-tuple-element.19), calls=%async_computation | async-start | bytes 32768 | tf_op jit(solution)/shard_map/all_to_all | solution.py:383

commit v5 on v4

--- a/solution.py
+++ b/solution.py
@@ -12,8 +12,8 @@
 BAND = 16
 ROWS = 4 * BAND
 TILE = 1024
-EARLY = 1152
-PART = 512
+EARLY = 1088
+PART = 256
 LIMIT = 24 << 20
 COST = pl.CostEstimate(flops=2_000_000_000, bytes_accessed=6_000_000, transcendentals=0)
 F32 = jnp.float32
@@ -230,99 +230,93 @@
     )(parts, cols)
 
 
-def upper_kernel(cols_ref, own_ref, upper_ref, bands_ref):
+def halves_times_turned(high, low, turned):
+    turned_high, turned_low = split(turned)
+    last = ((1,), (1,))
+    return mm(high, turned_high, last) + (mm(high, turned_low, last) + mm(low, turned_high, last))
+
+
+def upper_kernel(
+    cols_ref, own_ref, raw_ref, upper_high, upper_low, raw_high, raw_low, bands_ref, raw_tiles, sems
+):
+    count = sems.shape[0]
+    step = EARLY // count
+    loads = [
+        pltpu.make_async_copy(raw_ref.at[pl.ds(i * step, step)], raw_tiles.at[pl.ds(i * step, step)], sems.at[i])
+        for i in range(count)
+    ]
+    for load in loads:
+        load.start()
     upper = times_turned(cols_ref[...], turned_half(own_ref[:BAND, :], own_ref[BAND:, :], 1 - BAND))
-    upper_ref[...] = upper
     high, low = split(upper)
+    upper_high[...] = high
+    upper_low[...] = low
     rows = ((0,), (0,))
     cross = mm(high, low, rows)
     gram = mm(high, high, rows) + mm(low, low, rows) + (cross + cross.T)
     bands_ref[...] = jnp.concatenate(bands_of(gram, BAND), axis=0)
-
-
-def upper_half(cols, own):
+    for load in loads:
+        load.wait()
+    high, low = split(raw_tiles[...])
+    raw_high[...] = high
+    raw_low[...] = low
+
+
+def upper_half(cols, own, raw):
+    rows = cols.shape[0]
+    upper = jax.ShapeDtypeStruct((rows, BLK), BF16)
+    early = jax.ShapeDtypeStruct(raw.shape, BF16)
     return pl.pallas_call(
         upper_kernel,
-        in_specs=[VMEM_SPEC, VMEM_SPEC],
-        out_shape=(
-            jax.ShapeDtypeStruct((cols.shape[0], BLK), F32),
-            jax.ShapeDtypeStruct((BAND, BLK), F32),
-        ),
+        in_specs=[VMEM_SPEC, VMEM_SPEC, pl.BlockSpec(memory_space=pltpu.HBM)],
+        out_shape=(upper, upper, early, early, jax.ShapeDtypeStruct((BAND, BLK), F32)),
+        scratch_shapes=[pltpu.VMEM(raw.shape, F32), pltpu.SemaphoreType.DMA((2,))],
         cost_estimate=COST,
         compiler_params=PARAMS,
         name="upper_half",
-    )(cols, own)
-
-
-def lower_gram(upper, lower):
-    low_high, low_low = split(lower)
-    pair_high, pair_low = split(jnp.concatenate((upper, lower), axis=1))
+    )(cols, own, raw)
+
+
+def link_kernel(raw_high, raw_low, late_ref, upper_high, upper_low, uu_ref, pair_high, pair_low, bands_ref):
+    turned = turned_half(late_ref[:BAND, :], late_ref[BAND : 2 * BAND, :], 0)
+    early_high, early_low = split(halves_times_turned(raw_high[...], raw_low[...], turned))
+    late_high, late_low = split(late_ref[2 * BAND :, :])
+    pair_high[:, :BLK] = upper_high[...]
+    pair_low[:, :BLK] = upper_low[...]
+    pair_high[:EARLY, BLK:] = early_high
+    pair_low[:EARLY, BLK:] = early_low
+    pair_high[EARLY:, BLK:] = late_high
+    pair_low[EARLY:, BLK:] = late_low
+    high, low = pair_high[...], pair_low[...]
+    lower_high, lower_low = high[:, BLK:], low[:, BLK:]
     rows = ((0,), (0,))
-    return (
-        mm(low_high, pair_high, rows)
-        + mm(low_low, pair_low, rows)
-        + (mm(low_high, pair_low, rows) + mm(low_low, pair_high, rows))
+    gram = (
+        mm(lower_high, high, rows)
+        + mm(lower_low, low, rows)
+        + (mm(lower_high, low, rows) + mm(lower_low, high, rows))
     )
-
-
-def link_kernel(raw_ref, late_ref, upper_ref, uu_ref, pair_ref, bands_ref, turned_ref, total_ref):
-    step = pl.program_id(0)
-
-    @pl.when(step == 0)
-    def _():
-        turned_ref[...] = turned_half(late_ref[:BAND, :], late_ref[BAND : 2 * BAND, :], 0)
-        late = late_ref[2 * BAND :, :]
-        upper = upper_ref[EARLY:, :]
-        pair_ref[EARLY:, :BLK] = upper
-        pair_ref[EARLY:, BLK:] = late
-        total_ref[...] = lower_gram(upper, late)
-
-    tile = raw_ref.shape[0]
-    rows = pl.ds(pl.multiple_of(step * tile, 8), tile)
-    lower = times_turned(raw_ref[...], turned_ref[...])
-    upper = upper_ref[rows, :]
-    pair_ref[rows, :BLK] = upper
-    pair_ref[rows, BLK:] = lower
-    total_ref[...] += lower_gram(upper, lower)
-
-    @pl.when(step == pl.num_programs(0) - 1)
-    def _():
-        total = total_ref[...]
-        lu, ll = total[:, :BLK], total[:, BLK:]
-        bands_ref[:BAND, :] = uu_ref[...]
-        bands_ref[BAND:, :] = jnp.concatenate(
-            bands_of(lu.T, BAND) + bands_of(lu, BAND) + bands_of(ll, BAND), axis=0
-        )
-
-
-def link(raw, late, upper, uu):
-    rows = upper.shape[0]
+    lu, ll = gram[:, :BLK], gram[:, BLK:]
+    bands_ref[:BAND, :] = uu_ref[...]
+    bands_ref[BAND:, :] = jnp.concatenate(
+        bands_of(lu.T, BAND) + bands_of(lu, BAND) + bands_of(ll, BAND), axis=0
+    )
+
+
+def link(early, late, upper, uu):
+    rows = upper[0].shape[0]
+    pair = jax.ShapeDtypeStruct((rows, 2 * BLK), BF16)
     return pl.pallas_call(
         link_kernel,
-        grid=(2,),
-        in_specs=[
-            pl.BlockSpec((EARLY // 2, 2 * BLK), lambda i: (i, 0)),
-            pl.BlockSpec(late.shape, lambda i: (0, 0)),
-            pl.BlockSpec(upper.shape, lambda i: (0, 0)),
-            pl.BlockSpec(uu.shape, lambda i: (0, 0)),
-        ],
-        out_specs=(
-            pl.BlockSpec((rows, 2 * BLK), lambda i: (0, 0)),
-            pl.BlockSpec((ROWS, BLK), lambda i: (0, 0)),
-        ),
-        out_shape=(
-            jax.ShapeDtypeStruct((rows, 2 * BLK), F32),
-            jax.ShapeDtypeStruct((ROWS, BLK), F32),
-        ),
-        scratch_shapes=[pltpu.VMEM((BLK, 2 * BLK), F32), pltpu.VMEM((BLK, 2 * BLK), F32)],
+        in_specs=[VMEM_SPEC] * 6,
+        out_shape=(pair, pair, jax.ShapeDtypeStruct((ROWS, BLK), F32)),
         cost_estimate=COST,
         compiler_params=PARAMS,
         name="link",
-    )(raw, late, upper, uu)
+    )(*early, late, *upper, uu)
 
 
 def final_kernel(
-    entry_count, parts_ref, traces_ref, pair_ref, out_ref, tiles_ref, high_ref, low_ref, sems
+    entry_count, parts_ref, traces_ref, pair_high, pair_low, out_ref, tiles_ref, high_ref, low_ref, sems
 ):
     rms = jnp.sqrt(jnp.sum(summed(traces_ref), axis=1, keepdims=True) / entry_count)
     u_top, u_low, l_top, l_low = jacobi_bands(*blocks(summed(parts_ref)))
@@ -337,7 +331,7 @@
     stores = []
     for i in range(tiles_ref.shape[0]):
         rows = pl.ds(i * PART, PART)
-        high, low = split(pair_ref[rows, :])
+        high, low = pair_high[rows, :], pair_low[rows, :]
         tiles_ref[i] = mm(high, high_ref[...], last) + (
             mm(high, low_ref[...], last) + mm(low, high_ref[...], last)
         )
@@ -349,11 +343,11 @@
 
 
 def final(entry_count, parts, traces, pair):
-    rows = pair.shape[0]
+    rows = pair[0].shape[0]
     count = rows // PART
     return pl.pallas_call(
         functools.partial(final_kernel, entry_count),
-        in_specs=[VMEM_SPEC] * 3,
+        in_specs=[VMEM_SPEC] * 4,
         out_specs=pl.BlockSpec(memory_space=pltpu.HBM),
         out_shape=jax.ShapeDtypeStruct((rows, 2 * BLK), F32),
         scratch_shapes=[
@@ -364,7 +358,7 @@
         ],
         compiler_params=PARAMS,
         name="final",
-    )(parts, traces, pair)
+    )(parts, traces, *pair)
 
 
 def to_next(value):
@@ -381,8 +375,8 @@
     own, late, traces = jacobi(lax.all_gather(bands, "row"), activations, pairs)
     late = to_next(late)
     traces = lax.all_to_all(traces, "pair", 0, 0, tiled=True)
-    upper, uu = upper_half(activations, own)
-    pair, bands = link(raw, late, upper, uu)
+    upper_high, upper_low, early_high, early_low, uu = upper_half(activations, own, raw)
+    *pair, bands = link((early_high, early_low), late, (upper_high, upper_low), uu)
     bands, traces = lax.optimization_barrier((bands, traces))
     parts = lax.all_gather(bands, "row")
     return final(float(entry_count), parts, traces, pair)

time: 80.1 us -> 78.6 us (0.981)
  blocking collectives: 43.4 us -> 42 us
    all_gather x1, blocking collectives: 18 us -> 16.6 us  [body(): parts = lax.all_gather(bands, 'row')]
  transfers between devices with their start and end apart: 3 -> 3, of which waited for: 1 -> 1; matrix products, arithmetic and copies ran while one was open for 0% -> 0% of each run, Pallas kernels for 15% -> 14%
where the time goes in v5:
time: 78.6 us; the launch traced here: 78.3 us
  blocking collectives  42 us (53%)
  Pallas kernels  16.4 us (21%)
  starting transfers between devices  15.1 us (19%)
  waiting for transfers between devices  4.67 us (6%)
    all_gather x1, blocking collectives, body(): own, late, traces = jacobi(lax.all_gather(bands, 'row'), activations, pairs)  25.4 us
    all_gather x1, blocking collectives, body(): parts = lax.all_gather(bands, 'row')  16.6 us
    all_to_all x1, starting transfers between devices, body(): traces = lax.all_to_all(traces, 'pair', 0, 0, tiled=True)  7.88 us
    ppermute x2, starting transfers between devices, to_next(): lax.ppermute(value, 'pair', [(pair, (pair + 1) % count) for pair in range...  7.23 us
    ppermute x2, waiting for transfers between devices, to_next(): lax.ppermute(value, 'pair', [(pair, (pair + 1) % count) for pair in range...  4.67 us
    pallas_call x1, Pallas kernels, link(): pl.pallas_call(link_kernel, in_specs=[VMEM_SPEC] * 6, out_shape=(pair, pa...  3.84 us
    pallas_call x1, Pallas kernels, final(): pl.pallas_call(functools.partial(final_kernel, entry_count), in_specs=[VM...  3.83 us
    pallas_call x1, Pallas kernels, jacobi(): pl.pallas_call(jacobi_kernel, in_specs=[VMEM_SPEC, VMEM_SPEC], out_shape=...  3.2 us
  transfers between devices with their start and end apart: 3, of which 1 were waited for; matrix products, arithmetic and copies ran while one was open for 0% of the time, Pallas kernels for 14%

profile of v5, /device:TPU:1, one launch (start us, length us, event | category | flops | bytes accessed | tf_op | source)
XLA Modules:
  0.0 78.3 jit_solution(13379670651727169372)
XLA Ops:
  0.0 0.0 copy-start
  0.0 1.4 %early_rows.1 = f32[1088,256]{1,0:T(8,128)S(1)} custom-call(f32[2048,256]{1,0:T(8,128)} %cols_ref.7), custom_call_target="tpu_custom_call" | custom-call | tf_op jit(solution)/shard_map/early_rows/pallas_call | solution.py:185
  1.4 4.0 %collective-permute-start = (f32[1088,256]{1,0:T(8,128)S(1)}, f32[1088,256]{1,0:T(8,128)}, u32[]{:S(2)}, u32[]{:S(2)}) collective-permute-start(f32[1088,256]{1,0:T(8,128)S(1)} %early_rows.1), channel_id=1, source_target_pairs={{0,16},{16,32},{32,48},{48,64},{64,80},{80,96},{96,112},{112,128},... | collective-permute-start | bytes 3342344 | tf_op jit(solution)/shard_map/ppermute | solution.py:366
  5.4 0.0 copy-done
  5.5 1.4 %gram_bands.1 = f32[64,128]{1,0:T(8,128)S(1)} custom-call(f32[2048,256]{1,0:T(8,128)S(1)} %copy-done), custom_call_target="tpu_custom_call" | custom-call | tf_op jit(solution)/shard_map/gram_bands/pallas_call | solution.py:200
  6.9 25.4 %all-gather = f32[1024,128]{1,0:T(8,128)S(1)} all-gather(f32[64,128]{1,0:T(8,128)S(1)} %gram_bands.1), channel_id=2, replica_groups=mesh['pair'=32,'row'=16] {'row'}, dimensions={0}, use_global_device_ids=true | all-gather | bytes 557056 | tf_op jit(solution)/shard_map/all_gather | solution.py:375
  32.3 3.2 %jacobi.1 = (f32[32,128]{1,0:T(8,128)S(1)}, f32[992,128]{1,0:T(8,128)}, f32[32,1,128]{2,1,0:T(1,128)}) custom-call(f32[16,64,128]{2,1,0:T(8,128)S(1)} %bitcast.3, f32[2048,256]{1,0:T(8,128)S(1)} %copy-done), custom_call_target="tpu_custom_call" | custom-call | tf_op jit(solution)/shard_map/jacobi/pallas_call | solution.py:220
  35.5 3.2 %collective-permute-start.1 = (f32[992,128]{1,0:T(8,128)}, f32[992,128]{1,0:T(8,128)}, u32[]{:S(2)}, u32[]{:S(2)}) collective-permute-start(f32[992,128]{1,0:T(8,128)} %get-tuple-element.21), channel_id=1, source_target_pairs={{0,16},{16,32},{32,48},{48,64},{64,80},{80,96},{96,112},{112,128},... | collective-permute-start | bytes 1523720 | tf_op jit(solution)/shard_map/ppermute | solution.py:366
  38.7 7.9 %all-to-all-start = ((f32[32,1,128]{2,1,0:T(1,128)}), f32[32,1,128]{2,1,0:T(1,128)S(1)}, u32[]{:S(2)}, u32[]{:S(2)}) async-start(f32[32,1,128]{2,1,0:T(1,128)} %get-tuple-element.26), calls=%async_computation | async-start | bytes 32768 | tf_op jit(solution)/shard_map/all_to_all | solution.py:377
  46.6 0.0 collective-permute-done.raw_ref
  46.6 2.8 %upper_half.1 = (bf16[2048,128]{1,0:T(8,128)(2,1)S(1)}, bf16[2048,128]{1,0:T(8,128)(2,1)S(1)}, bf16[1088,256]{1,0:T(8,128)(2,1)S(1)}, bf16[1088,256]{1,0:T(8,128)(2,1)S(1)}, f32[16,128]{1,0:T(8,128)S(1)}) custom-call(f32[2048,256]{1,0:T(8,128)S(1)} %copy-done, f32[32,128]{1,0:T(8,128)S(1)} %get-tuple-element.18.own_ref, f32[1088,256]{1,0:T(8,128)} %collective-permute-done.raw_ref), custom_call_target="tpu_custom_call" | custom-call | flops 2000000000 | bytes 6000000 | tf_op jit(solution)/shard_map/upper_half/pallas_call | solution.py:269
  49.3 4.7 %collective-permute-done.1.late_ref = f32[992,128]{1,0:T(8,128)} collective-permute-done((f32[992,128]{1,0:T(8,128)}, f32[992,128]{1,0:T(8,128)}, u32[]{:S(2)}, u32[]{:S(2)}) %collective-permute-start.1) | collective-permute-done | bytes 507936 | tf_op jit(solution)/shard_map/ppermute | solution.py:366
  54.0 3.8 %link.1 = (bf16[2048,256]{1,0:T(8,128)(2,1)S(1)}, bf16[2048,256]{1,0:T(8,128)(2,1)S(1)}, f32[64,128]{1,0:T(8,128)S(1)}) custom-call(bf16[1088,256]{1,0:T(8,128)(2,1)S(1)} %get-tuple-element.19.raw_high, bf16[1088,256]{1,0:T(8,128)(2,1)S(1)} %get-tuple-element.20.raw_low, f32[992,128]{1,0:T(8,128)} %collective-permute-done.1.late_ref, ...), custom_call_target="tpu_custom_call" | custom-call | flops 2000000000 | bytes 6000000 | tf_op jit(solution)/shard_map/link/pallas_call | solution.py:308
  57.8 0.0 all-to-all-done.traces_ref
  57.9 16.6 %all-gather.1 = f32[1024,128]{1,0:T(8,128)S(1)} all-gather(f32[64,128]{1,0:T(8,128)S(1)} %get-tuple-element.27), channel_id=3, replica_groups=mesh['pair'=32,'row'=16] {'row'}, dimensions={0}, use_global_device_ids=true | all-gather | bytes 557056 | tf_op jit(solution)/shard_map/all_gather | solution.py:381
  74.5 3.8 %final.1 = f32[2048,256]{1,0:T(8,128)} custom-call(f32[16,64,128]{2,1,0:T(8,128)S(1)} %bitcast.2, f32[32,1,128]{2,1,0:T(1,128)S(1)} %all-to-all-done.traces_ref, bf16[2048,256]{1,0:T(8,128)(2,1)S(1)} %get-tuple-element.29.pair_high, bf16[2048,256]{1,0:T(8,128)(2,1)S(1)} %get-tuple-element.30.pair_low), custom_call_target="tpu_custom_call" | custom-call | tf_op jit(solution)/shard_map/final/pallas_call | solution.py:348
Async XLA Ops:
  0.0 5.4 %copy-start = (f32[2048,256]{1,0:T(8,128)S(1)}, f32[2048,256]{1,0:T(8,128)}, u32[]{:S(2)}) copy-start(f32[2048,256]{1,0:T(8,128)} %cols_ref.7) | copy-start | bytes 6291460
  1.4 45.2 %collective-permute-start = (f32[1088,256]{1,0:T(8,128)S(1)}, f32[1088,256]{1,0:T(8,128)}, u32[]{:S(2)}, u32[]{:S(2)}) collective-permute-start(f32[1088,256]{1,0:T(8,128)S(1)} %early_rows.1), channel_id=1, source_target_pairs={{0,16},{16,32},{32,48},{48,64},{64,80},{80,96},{96,112},{112,128},... | collective-permute-start | bytes 3342344 | tf_op jit(solution)/shard_map/ppermute | solution.py:366
  35.5 18.5 %collective-permute-start.1 = (f32[992,128]{1,0:T(8,128)}, f32[992,128]{1,0:T(8,128)}, u32[]{:S(2)}, u32[]{:S(2)}) collective-permute-start(f32[992,128]{1,0:T(8,128)} %get-tuple-element.21), channel_id=1, source_target_pairs={{0,16},{16,32},{32,48},{48,64},{64,80},{80,96},{96,112},{112,128},... | collective-permute-start | bytes 1523720 | tf_op jit(solution)/shard_map/ppermute | solution.py:366
  38.7 19.2 %all-to-all-start = ((f32[32,1,128]{2,1,0:T(1,128)}), f32[32,1,128]{2,1,0:T(1,128)S(1)}, u32[]{:S(2)}, u32[]{:S(2)}) async-start(f32[32,1,128]{2,1,0:T(1,128)} %get-tuple-element.26), calls=%async_computation | async-start | bytes 32768 | tf_op jit(solution)/shard_map/all_to_all | solution.py:377

commit v6 on v5

--- a/solution.py
+++ b/solution.py
@@ -209,21 +209,21 @@
 def jacobi_kernel(parts_ref, cols_ref, own_ref, late_ref, trace_ref):
     bands = summed(parts_ref)
     uu, ul, lu, ll = blocks(bands)
-    trace_ref[...] = jnp.broadcast_to((uu[:1] + ll[:1])[None], trace_ref.shape)
+    trace_ref[...] = uu[:8] + ll[:8]
     u_top, u_low, l_top, l_low = jacobi_bands(uu, ul, lu, ll)
     own_ref[...] = jnp.concatenate((u_top, u_low), axis=0)
     late_ref[: 2 * BAND, :] = jnp.concatenate((l_top, l_low), axis=0)
     late_ref[2 * BAND :, :] = times_turned(cols_ref[EARLY:, :], turned_half(l_top, l_low, 0))
 
 
-def jacobi(parts, cols, copies):
+def jacobi(parts, cols):
     return pl.pallas_call(
         jacobi_kernel,
         in_specs=[VMEM_SPEC, VMEM_SPEC],
         out_shape=(
             pltpu.VMEM((2 * BAND, BLK), F32),
             jax.ShapeDtypeStruct((2 * BAND + cols.shape[0] - EARLY, BLK), F32),
-            jax.ShapeDtypeStruct((copies, 1, BLK), F32),
+            jax.ShapeDtypeStruct((8, BLK), F32),
         ),
         compiler_params=PARAMS,
         name="jacobi",
@@ -277,12 +277,22 @@
     )(cols, own, raw)
 
 
-def link_kernel(raw_high, raw_low, late_ref, upper_high, upper_low, uu_ref, pair_high, pair_low, bands_ref):
-    turned = turned_half(late_ref[:BAND, :], late_ref[BAND : 2 * BAND, :], 0)
-    early_high, early_low = split(halves_times_turned(raw_high[...], raw_low[...], turned))
-    late_high, late_low = split(late_ref[2 * BAND :, :])
+def link_kernel(
+    raw_high, raw_low, late_ref, upper_high, upper_low, uu_ref, pair_high, pair_low, bands_ref, late_tiles, sems
+):
+    loads = []
+    for i, (first, size) in enumerate(((0, 2 * BAND), (2 * BAND, late_ref.shape[0] - 2 * BAND))):
+        rows = pl.ds(first, size)
+        load = pltpu.make_async_copy(late_ref.at[rows], late_tiles.at[rows], sems.at[i])
+        load.start()
+        loads.append(load)
     pair_high[:, :BLK] = upper_high[...]
     pair_low[:, :BLK] = upper_low[...]
+    loads[0].wait()
+    turned = turned_half(late_tiles[:BAND, :], late_tiles[BAND : 2 * BAND, :], 0)
+    early_high, early_low = split(halves_times_turned(raw_high[...], raw_low[...], turned))
+    loads[1].wait()
+    late_high, late_low = split(late_tiles[2 * BAND :, :])
     pair_high[:EARLY, BLK:] = early_high
     pair_low[:EARLY, BLK:] = early_low
     pair_high[EARLY:, BLK:] = late_high
@@ -307,8 +317,9 @@
     pair = jax.ShapeDtypeStruct((rows, 2 * BLK), BF16)
     return pl.pallas_call(
         link_kernel,
-        in_specs=[VMEM_SPEC] * 6,
+        in_specs=[VMEM_SPEC] * 2 + [pl.BlockSpec(memory_space=pltpu.HBM)] + [VMEM_SPEC] * 3,
         out_shape=(pair, pair, jax.ShapeDtypeStruct((ROWS, BLK), F32)),
+        scratch_shapes=[pltpu.VMEM(late.shape, F32), pltpu.SemaphoreType.DMA((2,))],
         cost_estimate=COST,
         compiler_params=PARAMS,
         name="link",
@@ -372,8 +383,9 @@
 
     raw = to_next(early_rows(activations))
     bands = gram_bands(activations)
-    own, late, traces = jacobi(lax.all_gather(bands, "row"), activations, pairs)
+    own, late, trace = jacobi(lax.all_gather(bands, "row"), activations)
     late = to_next(late)
+    traces = jnp.broadcast_to(trace[:1][None], (pairs, 1, BLK))
     traces = lax.all_to_all(traces, "pair", 0, 0, tiled=True)
     upper_high, upper_low, early_high, early_low, uu = upper_half(activations, own, raw)
     *pair, bands = link((early_high, early_low), late, (upper_high, upper_low), uu)

time: 78.6 us -> 78.4 us (level)
  transfers between devices with their start and end apart: 3 -> 3, of which waited for: 1 -> 1; matrix products, arithmetic and copies ran while one was open for 0% -> 1% of each run, Pallas kernels for 14% -> 14%
where the time goes in v6:
time: 78.4 us; the launch traced here: 78.1 us
  blocking collectives  42 us (54%)
  Pallas kernels  16.3 us (21%)
  starting transfers between devices  15.1 us (19%)
  waiting for transfers between devices  4.06 us (5%)
    all_gather x1, blocking collectives, body(): own, late, trace = jacobi(lax.all_gather(bands, 'row'), activations)  25.4 us
    all_gather x1, blocking collectives, body(): parts = lax.all_gather(bands, 'row')  16.6 us
    all_to_all x1, starting transfers between devices, body(): traces = lax.all_to_all(traces, 'pair', 0, 0, tiled=True)  7.87 us
    ppermute x2, starting transfers between devices, to_next(): lax.ppermute(value, 'pair', [(pair, (pair + 1) % count) for pair in range...  7.23 us
    ppermute x2, waiting for transfers between devices, to_next(): lax.ppermute(value, 'pair', [(pair, (pair + 1) % count) for pair in range...  4.06 us
    pallas_call x1, Pallas kernels, final(): pl.pallas_call(functools.partial(final_kernel, entry_count), in_specs=[VM...  3.83 us
    pallas_call x1, Pallas kernels, link(): pl.pallas_call(link_kernel, in_specs=[VMEM_SPEC] * 2 + [pl.BlockSpec(memo...  3.66 us
    pallas_call x1, Pallas kernels, jacobi(): pl.pallas_call(jacobi_kernel, in_specs=[VMEM_SPEC, VMEM_SPEC], out_shape=...  3.2 us
  transfers between devices with their start and end apart: 3, of which 1 were waited for; matrix products, arithmetic and copies ran while one was open for 1% of the time, Pallas kernels for 14%

profile of v6, /device:TPU:1, one launch (start us, length us, event | category | flops | bytes accessed | tf_op | source)
XLA Modules:
  0.0 78.1 jit_solution(11994018267946854478)
XLA Ops:
  0.0 0.0 copy-start
  0.0 1.4 %early_rows.1 = f32[1088,256]{1,0:T(8,128)S(1)} custom-call(f32[2048,256]{1,0:T(8,128)} %cols_ref.7), custom_call_target="tpu_custom_call" | custom-call | tf_op jit(solution)/shard_map/early_rows/pallas_call | solution.py:185
  1.4 4.0 %collective-permute-start = (f32[1088,256]{1,0:T(8,128)S(1)}, f32[1088,256]{1,0:T(8,128)}, u32[]{:S(2)}, u32[]{:S(2)}) collective-permute-start(f32[1088,256]{1,0:T(8,128)S(1)} %early_rows.1), channel_id=1, source_target_pairs={{0,16},{16,32},{32,48},{48,64},{64,80},{80,96},{96,112},{112,128},... | collective-permute-start | bytes 3342344 | tf_op jit(solution)/shard_map/ppermute | solution.py:377
  5.4 0.0 copy-done
  5.5 1.4 %gram_bands.1 = f32[64,128]{1,0:T(8,128)S(1)} custom-call(f32[2048,256]{1,0:T(8,128)S(1)} %copy-done), custom_call_target="tpu_custom_call" | custom-call | tf_op jit(solution)/shard_map/gram_bands/pallas_call | solution.py:200
  6.9 25.4 %all-gather = f32[1024,128]{1,0:T(8,128)S(1)} all-gather(f32[64,128]{1,0:T(8,128)S(1)} %gram_bands.1), channel_id=2, replica_groups=mesh['pair'=32,'row'=16] {'row'}, dimensions={0}, use_global_device_ids=true | all-gather | bytes 557056 | tf_op jit(solution)/shard_map/all_gather | solution.py:386
  32.3 3.2 %jacobi.1 = (f32[32,128]{1,0:T(8,128)S(1)}, f32[992,128]{1,0:T(8,128)}, f32[8,128]{1,0:T(8,128)S(1)}) custom-call(f32[16,64,128]{2,1,0:T(8,128)S(1)} %bitcast.5, f32[2048,256]{1,0:T(8,128)S(1)} %copy-done), custom_call_target="tpu_custom_call" | custom-call | tf_op jit(solution)/shard_map/jacobi/pallas_call | solution.py:220
  35.5 3.2 %collective-permute-start.1 = (f32[992,128]{1,0:T(8,128)}, f32[992,128]{1,0:T(8,128)}, u32[]{:S(2)}, u32[]{:S(2)}) collective-permute-start(f32[992,128]{1,0:T(8,128)} %get-tuple-element.21), channel_id=1, source_target_pairs={{0,16},{16,32},{32,48},{48,64},{64,80},{80,96},{96,112},{112,128},... | collective-permute-start | bytes 1523720 | tf_op jit(solution)/shard_map/ppermute | solution.py:377
  38.7 0.6 broadcast_in_dim.9
  39.3 7.9 %all-to-all-start = ((f32[32,1,128]{2,1,0:T(1,128)}), f32[32,1,128]{2,1,0:T(1,128)S(1)}, u32[]{:S(2)}, u32[]{:S(2)}) async-start(f32[32,1,128]{2,1,0:T(1,128)} %broadcast_in_dim.9), calls=%async_computation | async-start | bytes 32768 | tf_op jit(solution)/shard_map/all_to_all | solution.py:389
  47.2 0.0 collective-permute-done.raw_ref
  47.2 2.8 %upper_half.1 = (bf16[2048,128]{1,0:T(8,128)(2,1)S(1)}, bf16[2048,128]{1,0:T(8,128)(2,1)S(1)}, bf16[1088,256]{1,0:T(8,128)(2,1)S(1)}, bf16[1088,256]{1,0:T(8,128)(2,1)S(1)}, f32[16,128]{1,0:T(8,128)S(1)}) custom-call(f32[2048,256]{1,0:T(8,128)S(1)} %copy-done, f32[32,128]{1,0:T(8,128)S(1)} %get-tuple-element.18.own_ref, f32[1088,256]{1,0:T(8,128)} %collective-permute-done.raw_ref), custom_call_target="tpu_custom_call" | custom-call | flops 2000000000 | bytes 6000000 | tf_op jit(solution)/shard_map/upper_half/pallas_call | solution.py:269
  49.9 4.1 %collective-permute-done.1.late_ref = f32[992,128]{1,0:T(8,128)} collective-permute-done((f32[992,128]{1,0:T(8,128)}, f32[992,128]{1,0:T(8,128)}, u32[]{:S(2)}, u32[]{:S(2)}) %collective-permute-start.1) | collective-permute-done | bytes 507936 | tf_op jit(solution)/shard_map/ppermute | solution.py:377
  54.0 3.7 %link.1 = (bf16[2048,256]{1,0:T(8,128)(2,1)S(1)}, bf16[2048,256]{1,0:T(8,128)(2,1)S(1)}, f32[64,128]{1,0:T(8,128)S(1)}) custom-call(bf16[1088,256]{1,0:T(8,128)(2,1)S(1)} %get-tuple-element.19.raw_high, bf16[1088,256]{1,0:T(8,128)(2,1)S(1)} %get-tuple-element.20.raw_low, f32[992,128]{1,0:T(8,128)} %collective-permute-done.1.late_ref, ...), custom_call_target="tpu_custom_call" | custom-call | flops 2000000000 | bytes 6000000 | tf_op jit(solution)/shard_map/link/pallas_call | solution.py:318
  57.7 0.0 all-to-all-done.traces_ref
  57.7 16.6 %all-gather.1 = f32[1024,128]{1,0:T(8,128)S(1)} all-gather(f32[64,128]{1,0:T(8,128)S(1)} %get-tuple-element.27), channel_id=3, replica_groups=mesh['pair'=32,'row'=16] {'row'}, dimensions={0}, use_global_device_ids=true | all-gather | bytes 557056 | tf_op jit(solution)/shard_map/all_gather | solution.py:393
  74.3 3.8 %final.1 = f32[2048,256]{1,0:T(8,128)} custom-call(f32[16,64,128]{2,1,0:T(8,128)S(1)} %bitcast.4, f32[32,1,128]{2,1,0:T(1,128)S(1)} %all-to-all-done.traces_ref, bf16[2048,256]{1,0:T(8,128)(2,1)S(1)} %get-tuple-element.29.pair_high, bf16[2048,256]{1,0:T(8,128)(2,1)S(1)} %get-tuple-element.30.pair_low), custom_call_target="tpu_custom_call" | custom-call | tf_op jit(solution)/shard_map/final/pallas_call | solution.py:359
  (1 shorter events, 0.0 us)
Async XLA Ops:
  0.0 5.4 %copy-start = (f32[2048,256]{1,0:T(8,128)S(1)}, f32[2048,256]{1,0:T(8,128)}, u32[]{:S(2)}) copy-start(f32[2048,256]{1,0:T(8,128)} %cols_ref.7) | copy-start | bytes 6291460
  1.4 45.8 %collective-permute-start = (f32[1088,256]{1,0:T(8,128)S(1)}, f32[1088,256]{1,0:T(8,128)}, u32[]{:S(2)}, u32[]{:S(2)}) collective-permute-start(f32[1088,256]{1,0:T(8,128)S(1)} %early_rows.1), channel_id=1, source_target_pairs={{0,16},{16,32},{32,48},{48,64},{64,80},{80,96},{96,112},{112,128},... | collective-permute-start | bytes 3342344 | tf_op jit(solution)/shard_map/ppermute | solution.py:377
  35.5 18.5 %collective-permute-start.1 = (f32[992,128]{1,0:T(8,128)}, f32[992,128]{1,0:T(8,128)}, u32[]{:S(2)}, u32[]{:S(2)}) collective-permute-start(f32[992,128]{1,0:T(8,128)} %get-tuple-element.21), channel_id=1, source_target_pairs={{0,16},{16,32},{32,48},{48,64},{64,80},{80,96},{96,112},{112,128},... | collective-permute-start | bytes 1523720 | tf_op jit(solution)/shard_map/ppermute | solution.py:377
  39.3 18.4 %all-to-all-start = ((f32[32,1,128]{2,1,0:T(1,128)}), f32[32,1,128]{2,1,0:T(1,128)S(1)}, u32[]{:S(2)}, u32[]{:S(2)}) async-start(f32[32,1,128]{2,1,0:T(1,128)} %broadcast_in_dim.9), calls=%async_computation | async-start | bytes 32768 | tf_op jit(solution)/shard_map/all_to_all | solution.py:389

commit v7 on v5

--- a/solution.py
+++ b/solution.py
@@ -12,7 +12,7 @@
 BAND = 16
 ROWS = 4 * BAND
 TILE = 1024
-EARLY = 1088
+EARLY = 1056
 PART = 256
 LIMIT = 24 << 20
 COST = pl.CostEstimate(flops=2_000_000_000, bytes_accessed=6_000_000, transcendentals=0)
@@ -187,7 +187,7 @@
         in_specs=[pl.BlockSpec(memory_space=pltpu.HBM)],
         out_specs=VMEM_SPEC,
         out_shape=pltpu.VMEM((EARLY, 2 * BLK), F32),
-        scratch_shapes=[pltpu.SemaphoreType.DMA((4,))],
+        scratch_shapes=[pltpu.SemaphoreType.DMA((6,))],
         name="early_rows",
     )(cols)
 

time: 78.6 us -> 79 us (level)
  no operation moved by 1% of the time
where the time goes in v7:
time: 79 us; the launch traced here: 78.8 us
  blocking collectives  42 us (53%)
  Pallas kernels  16.5 us (21%)
  starting transfers between devices  15.1 us (19%)
  waiting for transfers between devices  5.03 us (6%)
    all_gather x1, blocking collectives, body(): own, late, traces = jacobi(lax.all_gather(bands, 'row'), activations, pairs)  25.4 us
    all_gather x1, blocking collectives, body(): parts = lax.all_gather(bands, 'row')  16.6 us
    all_to_all x1, starting transfers between devices, body(): traces = lax.all_to_all(traces, 'pair', 0, 0, tiled=True)  7.88 us
    ppermute x2, starting transfers between devices, to_next(): lax.ppermute(value, 'pair', [(pair, (pair + 1) % count) for pair in range...  7.23 us
    ppermute x2, waiting for transfers between devices, to_next(): lax.ppermute(value, 'pair', [(pair, (pair + 1) % count) for pair in range...  5.02 us
    pallas_call x1, Pallas kernels, final(): pl.pallas_call(functools.partial(final_kernel, entry_count), in_specs=[VM...  3.83 us
    pallas_call x1, Pallas kernels, link(): pl.pallas_call(link_kernel, in_specs=[VMEM_SPEC] * 6, out_shape=(pair, pa...  3.81 us
    pallas_call x1, Pallas kernels, jacobi(): pl.pallas_call(jacobi_kernel, in_specs=[VMEM_SPEC, VMEM_SPEC], out_shape=...  3.22 us
  transfers between devices with their start and end apart: 3, of which 1 were waited for; matrix products, arithmetic and copies ran while one was open for 0% of the time, Pallas kernels for 14%

profile of v7, /device:TPU:1, one launch (start us, length us, event | category | flops | bytes accessed | tf_op | source)
XLA Modules:
  0.0 78.8 jit_solution(4929170988070406719)
XLA Ops:
  0.0 0.0 copy-start
  0.0 1.5 %early_rows.1 = f32[1056,256]{1,0:T(8,128)S(1)} custom-call(f32[2048,256]{1,0:T(8,128)} %cols_ref.7), custom_call_target="tpu_custom_call" | custom-call | tf_op jit(solution)/shard_map/early_rows/pallas_call | solution.py:185
  1.5 4.0 %collective-permute-start = (f32[1056,256]{1,0:T(8,128)S(1)}, f32[1056,256]{1,0:T(8,128)}, u32[]{:S(2)}, u32[]{:S(2)}) collective-permute-start(f32[1056,256]{1,0:T(8,128)S(1)} %early_rows.1), channel_id=1, source_target_pairs={{0,16},{16,32},{32,48},{48,64},{64,80},{80,96},{96,112},{112,128},... | collective-permute-start | bytes 3244040 | tf_op jit(solution)/shard_map/ppermute | solution.py:366
  5.5 0.0 copy-done
  5.6 1.4 %gram_bands.1 = f32[64,128]{1,0:T(8,128)S(1)} custom-call(f32[2048,256]{1,0:T(8,128)S(1)} %copy-done), custom_call_target="tpu_custom_call" | custom-call | tf_op jit(solution)/shard_map/gram_bands/pallas_call | solution.py:200
  7.0 25.4 %all-gather = f32[1024,128]{1,0:T(8,128)S(1)} all-gather(f32[64,128]{1,0:T(8,128)S(1)} %gram_bands.1), channel_id=2, replica_groups=mesh['pair'=32,'row'=16] {'row'}, dimensions={0}, use_global_device_ids=true | all-gather | bytes 557056 | tf_op jit(solution)/shard_map/all_gather | solution.py:375
  32.4 3.2 %jacobi.1 = (f32[32,128]{1,0:T(8,128)S(1)}, f32[1024,128]{1,0:T(8,128)}, f32[32,1,128]{2,1,0:T(1,128)}) custom-call(f32[16,64,128]{2,1,0:T(8,128)S(1)} %bitcast.3, f32[2048,256]{1,0:T(8,128)S(1)} %copy-done), custom_call_target="tpu_custom_call" | custom-call | tf_op jit(solution)/shard_map/jacobi/pallas_call | solution.py:220
  35.6 3.2 %collective-permute-start.1 = (f32[1024,128]{1,0:T(8,128)}, f32[1024,128]{1,0:T(8,128)}, u32[]{:S(2)}, u32[]{:S(2)}) collective-permute-start(f32[1024,128]{1,0:T(8,128)} %get-tuple-element.21), channel_id=1, source_target_pairs={{0,16},{16,32},{32,48},{48,64},{64,80},{80,96},{96,112},{112,128},... | collective-permute-start | bytes 1572872 | tf_op jit(solution)/shard_map/ppermute | solution.py:366
  38.8 7.9 %all-to-all-start = ((f32[32,1,128]{2,1,0:T(1,128)}), f32[32,1,128]{2,1,0:T(1,128)S(1)}, u32[]{:S(2)}, u32[]{:S(2)}) async-start(f32[32,1,128]{2,1,0:T(1,128)} %get-tuple-element.26), calls=%async_computation | async-start | bytes 32768 | tf_op jit(solution)/shard_map/all_to_all | solution.py:377
  46.7 0.0 collective-permute-done.raw_ref
  46.7 2.8 %upper_half.1 = (bf16[2048,128]{1,0:T(8,128)(2,1)S(1)}, bf16[2048,128]{1,0:T(8,128)(2,1)S(1)}, bf16[1056,256]{1,0:T(8,128)(2,1)S(1)}, bf16[1056,256]{1,0:T(8,128)(2,1)S(1)}, f32[16,128]{1,0:T(8,128)S(1)}) custom-call(f32[2048,256]{1,0:T(8,128)S(1)} %copy-done, f32[32,128]{1,0:T(8,128)S(1)} %get-tuple-element.18.own_ref, f32[1056,256]{1,0:T(8,128)} %collective-permute-done.raw_ref), custom_call_target="tpu_custom_call" | custom-call | flops 2000000000 | bytes 6000000 | tf_op jit(solution)/shard_map/upper_half/pallas_call | solution.py:269
  49.5 5.0 %collective-permute-done.1.late_ref = f32[1024,128]{1,0:T(8,128)} collective-permute-done((f32[1024,128]{1,0:T(8,128)}, f32[1024,128]{1,0:T(8,128)}, u32[]{:S(2)}, u32[]{:S(2)}) %collective-permute-start.1) | collective-permute-done | bytes 524320 | tf_op jit(solution)/shard_map/ppermute | solution.py:366
  54.5 3.8 %link.1 = (bf16[2048,256]{1,0:T(8,128)(2,1)S(1)}, bf16[2048,256]{1,0:T(8,128)(2,1)S(1)}, f32[64,128]{1,0:T(8,128)S(1)}) custom-call(bf16[1056,256]{1,0:T(8,128)(2,1)S(1)} %get-tuple-element.19.raw_high, bf16[1056,256]{1,0:T(8,128)(2,1)S(1)} %get-tuple-element.20.raw_low, f32[1024,128]{1,0:T(8,128)} %collective-permute-done.1.late_ref, ...), custom_call_target="tpu_custom_call" | custom-call | flops 2000000000 | bytes 6000000 | tf_op jit(solution)/shard_map/link/pallas_call | solution.py:308
  58.3 0.0 all-to-all-done.traces_ref
  58.3 16.6 %all-gather.1 = f32[1024,128]{1,0:T(8,128)S(1)} all-gather(f32[64,128]{1,0:T(8,128)S(1)} %get-tuple-element.27), channel_id=3, replica_groups=mesh['pair'=32,'row'=16] {'row'}, dimensions={0}, use_global_device_ids=true | all-gather | bytes 557056 | tf_op jit(solution)/shard_map/all_gather | solution.py:381
  74.9 3.8 %final.1 = f32[2048,256]{1,0:T(8,128)} custom-call(f32[16,64,128]{2,1,0:T(8,128)S(1)} %bitcast.2, f32[32,1,128]{2,1,0:T(1,128)S(1)} %all-to-all-done.traces_ref, bf16[2048,256]{1,0:T(8,128)(2,1)S(1)} %get-tuple-element.29.pair_high, bf16[2048,256]{1,0:T(8,128)(2,1)S(1)} %get-tuple-element.30.pair_low), custom_call_target="tpu_custom_call" | custom-call | tf_op jit(solution)/shard_map/final/pallas_call | solution.py:348
Async XLA Ops:
  0.0 5.5 %copy-start = (f32[2048,256]{1,0:T(8,128)S(1)}, f32[2048,256]{1,0:T(8,128)}, u32[]{:S(2)}) copy-start(f32[2048,256]{1,0:T(8,128)} %cols_ref.7) | copy-start | bytes 6291460
  1.5 45.2 %collective-permute-start = (f32[1056,256]{1,0:T(8,128)S(1)}, f32[1056,256]{1,0:T(8,128)}, u32[]{:S(2)}, u32[]{:S(2)}) collective-permute-start(f32[1056,256]{1,0:T(8,128)S(1)} %early_rows.1), channel_id=1, source_target_pairs={{0,16},{16,32},{32,48},{48,64},{64,80},{80,96},{96,112},{112,128},... | collective-permute-start | bytes 3244040 | tf_op jit(solution)/shard_map/ppermute | solution.py:366
  35.6 18.9 %collective-permute-start.1 = (f32[1024,128]{1,0:T(8,128)}, f32[1024,128]{1,0:T(8,128)}, u32[]{:S(2)}, u32[]{:S(2)}) collective-permute-start(f32[1024,128]{1,0:T(8,128)} %get-tuple-element.21), channel_id=1, source_target_pairs={{0,16},{16,32},{32,48},{48,64},{64,80},{80,96},{96,112},{112,128},... | collective-permute-start | bytes 1572872 | tf_op jit(solution)/shard_map/ppermute | solution.py:366
  38.8 19.5 %all-to-all-start = ((f32[32,1,128]{2,1,0:T(1,128)}), f32[32,1,128]{2,1,0:T(1,128)S(1)}, u32[]{:S(2)}, u32[]{:S(2)}) async-start(f32[32,1,128]{2,1,0:T(1,128)} %get-tuple-element.26), calls=%async_computation | async-start | bytes 32768 | tf_op jit(solution)/shard_map/all_to_all | solution.py:377

commit v8 on v6

--- a/solution.py
+++ b/solution.py
@@ -209,21 +209,21 @@
 def jacobi_kernel(parts_ref, cols_ref, own_ref, late_ref, trace_ref):
     bands = summed(parts_ref)
     uu, ul, lu, ll = blocks(bands)
-    trace_ref[...] = uu[:8] + ll[:8]
+    trace_ref[...] = jnp.broadcast_to((uu[:1] + ll[:1])[None], trace_ref.shape)
     u_top, u_low, l_top, l_low = jacobi_bands(uu, ul, lu, ll)
     own_ref[...] = jnp.concatenate((u_top, u_low), axis=0)
     late_ref[: 2 * BAND, :] = jnp.concatenate((l_top, l_low), axis=0)
     late_ref[2 * BAND :, :] = times_turned(cols_ref[EARLY:, :], turned_half(l_top, l_low, 0))
 
 
-def jacobi(parts, cols):
+def jacobi(parts, cols, copies):
     return pl.pallas_call(
         jacobi_kernel,
         in_specs=[VMEM_SPEC, VMEM_SPEC],
         out_shape=(
             pltpu.VMEM((2 * BAND, BLK), F32),
             jax.ShapeDtypeStruct((2 * BAND + cols.shape[0] - EARLY, BLK), F32),
-            jax.ShapeDtypeStruct((8, BLK), F32),
+            jax.ShapeDtypeStruct((copies, 1, BLK), F32),
         ),
         compiler_params=PARAMS,
         name="jacobi",
@@ -383,9 +383,8 @@
 
     raw = to_next(early_rows(activations))
     bands = gram_bands(activations)
-    own, late, trace = jacobi(lax.all_gather(bands, "row"), activations)
+    own, late, traces = jacobi(lax.all_gather(bands, "row"), activations, pairs)
     late = to_next(late)
-    traces = jnp.broadcast_to(trace[:1][None], (pairs, 1, BLK))
     traces = lax.all_to_all(traces, "pair", 0, 0, tiled=True)
     upper_high, upper_low, early_high, early_low, uu = upper_half(activations, own, raw)
     *pair, bands = link((early_high, early_low), late, (upper_high, upper_low), uu)

time: 78.4 us -> 78.4 us (level)
  transfers between devices with their start and end apart: 3 -> 3, of which waited for: 1 -> 1; matrix products, arithmetic and copies ran while one was open for 1% -> 0% of each run, Pallas kernels for 14% -> 14%
where the time goes in v8:
time: 78.4 us; the launch traced here: 78.1 us
  blocking collectives  42 us (54%)
  Pallas kernels  16.3 us (21%)
  starting transfers between devices  15.1 us (19%)
  waiting for transfers between devices  4.67 us (6%)
    all_gather x1, blocking collectives, body(): own, late, traces = jacobi(lax.all_gather(bands, 'row'), activations, pairs)  25.4 us
    all_gather x1, blocking collectives, body(): parts = lax.all_gather(bands, 'row')  16.6 us
    all_to_all x1, starting transfers between devices, body(): traces = lax.all_to_all(traces, 'pair', 0, 0, tiled=True)  7.88 us
    ppermute x2, starting transfers between devices, to_next(): lax.ppermute(value, 'pair', [(pair, (pair + 1) % count) for pair in range...  7.23 us
    ppermute x2, waiting for transfers between devices, to_next(): lax.ppermute(value, 'pair', [(pair, (pair + 1) % count) for pair in range...  4.67 us
    pallas_call x1, Pallas kernels, final(): pl.pallas_call(functools.partial(final_kernel, entry_count), in_specs=[VM...  3.83 us
    pallas_call x1, Pallas kernels, link(): pl.pallas_call(link_kernel, in_specs=[VMEM_SPEC] * 2 + [pl.BlockSpec(memo...  3.66 us
    pallas_call x1, Pallas kernels, jacobi(): pl.pallas_call(jacobi_kernel, in_specs=[VMEM_SPEC, VMEM_SPEC], out_shape=...  3.2 us
  transfers between devices with their start and end apart: 3, of which 1 were waited for; matrix products, arithmetic and copies ran while one was open for 0% of the time, Pallas kernels for 14%

profile of v8, /device:TPU:1, one launch (start us, length us, event | category | flops | bytes accessed | tf_op | source)
XLA Modules:
  0.0 78.1 jit_solution(14676573695637536438)
XLA Ops:
  0.0 0.0 copy-start
  0.0 1.4 %early_rows.1 = f32[1088,256]{1,0:T(8,128)S(1)} custom-call(f32[2048,256]{1,0:T(8,128)} %cols_ref.7), custom_call_target="tpu_custom_call" | custom-call | tf_op jit(solution)/shard_map/early_rows/pallas_call | solution.py:185
  1.4 4.0 %collective-permute-start = (f32[1088,256]{1,0:T(8,128)S(1)}, f32[1088,256]{1,0:T(8,128)}, u32[]{:S(2)}, u32[]{:S(2)}) collective-permute-start(f32[1088,256]{1,0:T(8,128)S(1)} %early_rows.1), channel_id=1, source_target_pairs={{0,16},{16,32},{32,48},{48,64},{64,80},{80,96},{96,112},{112,128},... | collective-permute-start | bytes 3342344 | tf_op jit(solution)/shard_map/ppermute | solution.py:377
  5.4 0.0 copy-done
  5.5 1.4 %gram_bands.1 = f32[64,128]{1,0:T(8,128)S(1)} custom-call(f32[2048,256]{1,0:T(8,128)S(1)} %copy-done), custom_call_target="tpu_custom_call" | custom-call | tf_op jit(solution)/shard_map/gram_bands/pallas_call | solution.py:200
  6.9 25.4 %all-gather = f32[1024,128]{1,0:T(8,128)S(1)} all-gather(f32[64,128]{1,0:T(8,128)S(1)} %gram_bands.1), channel_id=2, replica_groups=mesh['pair'=32,'row'=16] {'row'}, dimensions={0}, use_global_device_ids=true | all-gather | bytes 557056 | tf_op jit(solution)/shard_map/all_gather | solution.py:386
  32.3 3.2 %jacobi.1 = (f32[32,128]{1,0:T(8,128)S(1)}, f32[992,128]{1,0:T(8,128)}, f32[32,1,128]{2,1,0:T(1,128)}) custom-call(f32[16,64,128]{2,1,0:T(8,128)S(1)} %bitcast.3, f32[2048,256]{1,0:T(8,128)S(1)} %copy-done), custom_call_target="tpu_custom_call" | custom-call | tf_op jit(solution)/shard_map/jacobi/pallas_call | solution.py:220
  35.5 3.2 %collective-permute-start.1 = (f32[992,128]{1,0:T(8,128)}, f32[992,128]{1,0:T(8,128)}, u32[]{:S(2)}, u32[]{:S(2)}) collective-permute-start(f32[992,128]{1,0:T(8,128)} %get-tuple-element.21), channel_id=1, source_target_pairs={{0,16},{16,32},{32,48},{48,64},{64,80},{80,96},{96,112},{112,128},... | collective-permute-start | bytes 1523720 | tf_op jit(solution)/shard_map/ppermute | solution.py:377
  38.7 7.9 %all-to-all-start = ((f32[32,1,128]{2,1,0:T(1,128)}), f32[32,1,128]{2,1,0:T(1,128)S(1)}, u32[]{:S(2)}, u32[]{:S(2)}) async-start(f32[32,1,128]{2,1,0:T(1,128)} %get-tuple-element.26), calls=%async_computation | async-start | bytes 32768 | tf_op jit(solution)/shard_map/all_to_all | solution.py:388
  46.6 0.0 collective-permute-done.raw_ref
  46.6 2.8 %upper_half.1 = (bf16[2048,128]{1,0:T(8,128)(2,1)S(1)}, bf16[2048,128]{1,0:T(8,128)(2,1)S(1)}, bf16[1088,256]{1,0:T(8,128)(2,1)S(1)}, bf16[1088,256]{1,0:T(8,128)(2,1)S(1)}, f32[16,128]{1,0:T(8,128)S(1)}) custom-call(f32[2048,256]{1,0:T(8,128)S(1)} %copy-done, f32[32,128]{1,0:T(8,128)S(1)} %get-tuple-element.18.own_ref, f32[1088,256]{1,0:T(8,128)} %collective-permute-done.raw_ref), custom_call_target="tpu_custom_call" | custom-call | flops 2000000000 | bytes 6000000 | tf_op jit(solution)/shard_map/upper_half/pallas_call | solution.py:269
  49.3 4.7 %collective-permute-done.1.late_ref = f32[992,128]{1,0:T(8,128)} collective-permute-done((f32[992,128]{1,0:T(8,128)}, f32[992,128]{1,0:T(8,128)}, u32[]{:S(2)}, u32[]{:S(2)}) %collective-permute-start.1) | collective-permute-done | bytes 507936 | tf_op jit(solution)/shard_map/ppermute | solution.py:377
  54.0 3.7 %link.1 = (bf16[2048,256]{1,0:T(8,128)(2,1)S(1)}, bf16[2048,256]{1,0:T(8,128)(2,1)S(1)}, f32[64,128]{1,0:T(8,128)S(1)}) custom-call(bf16[1088,256]{1,0:T(8,128)(2,1)S(1)} %get-tuple-element.19.raw_high, bf16[1088,256]{1,0:T(8,128)(2,1)S(1)} %get-tuple-element.20.raw_low, f32[992,128]{1,0:T(8,128)} %collective-permute-done.1.late_ref, ...), custom_call_target="tpu_custom_call" | custom-call | flops 2000000000 | bytes 6000000 | tf_op jit(solution)/shard_map/link/pallas_call | solution.py:318
  57.7 0.0 all-to-all-done.traces_ref
  57.7 16.6 %all-gather.1 = f32[1024,128]{1,0:T(8,128)S(1)} all-gather(f32[64,128]{1,0:T(8,128)S(1)} %get-tuple-element.27), channel_id=3, replica_groups=mesh['pair'=32,'row'=16] {'row'}, dimensions={0}, use_global_device_ids=true | all-gather | bytes 557056 | tf_op jit(solution)/shard_map/all_gather | solution.py:392
  74.3 3.8 %final.1 = f32[2048,256]{1,0:T(8,128)} custom-call(f32[16,64,128]{2,1,0:T(8,128)S(1)} %bitcast.2, f32[32,1,128]{2,1,0:T(1,128)S(1)} %all-to-all-done.traces_ref, bf16[2048,256]{1,0:T(8,128)(2,1)S(1)} %get-tuple-element.29.pair_high, bf16[2048,256]{1,0:T(8,128)(2,1)S(1)} %get-tuple-element.30.pair_low), custom_call_target="tpu_custom_call" | custom-call | tf_op jit(solution)/shard_map/final/pallas_call | solution.py:359
Async XLA Ops:
  0.0 5.4 %copy-start = (f32[2048,256]{1,0:T(8,128)S(1)}, f32[2048,256]{1,0:T(8,128)}, u32[]{:S(2)}) copy-start(f32[2048,256]{1,0:T(8,128)} %cols_ref.7) | copy-start | bytes 6291460
  1.4 45.2 %collective-permute-start = (f32[1088,256]{1,0:T(8,128)S(1)}, f32[1088,256]{1,0:T(8,128)}, u32[]{:S(2)}, u32[]{:S(2)}) collective-permute-start(f32[1088,256]{1,0:T(8,128)S(1)} %early_rows.1), channel_id=1, source_target_pairs={{0,16},{16,32},{32,48},{48,64},{64,80},{80,96},{96,112},{112,128},... | collective-permute-start | bytes 3342344 | tf_op jit(solution)/shard_map/ppermute | solution.py:377
  35.5 18.5 %collective-permute-start.1 = (f32[992,128]{1,0:T(8,128)}, f32[992,128]{1,0:T(8,128)}, u32[]{:S(2)}, u32[]{:S(2)}) collective-permute-start(f32[992,128]{1,0:T(8,128)} %get-tuple-element.21), channel_id=1, source_target_pairs={{0,16},{16,32},{32,48},{48,64},{64,80},{80,96},{96,112},{112,128},... | collective-permute-start | bytes 1523720 | tf_op jit(solution)/shard_map/ppermute | solution.py:377
  38.7 19.0 %all-to-all-start = ((f32[32,1,128]{2,1,0:T(1,128)}), f32[32,1,128]{2,1,0:T(1,128)S(1)}, u32[]{:S(2)}, u32[]{:S(2)}) async-start(f32[32,1,128]{2,1,0:T(1,128)} %get-tuple-element.26), calls=%async_computation | async-start | bytes 32768 | tf_op jit(solution)/shard_map/all_to_all | solution.py:388
